TPU v7x, 32 devices: a whole 2x2x4 slice. The times are simulated.
32 devices in a mesh: comp: 16 (over z, y, core), grp: 2 (over x).
Axes of the slice: x: 2, y: 2, z: 4, core: 2. Of those that a mesh axis runs over, the one named last changes fastest.
Arguments:
- spectrum: float32 [1152, 16, 256], P('comp', 'grp'), may hold values from 0.1 to 1
- group_speed: float32 [2, 1152], replicated, may hold values from -0.25 to 0.25
- sea_mask: int32 [16, 256], P('grp'), may hold values 0 or 1
- quad_index: int32 [4, 1152], replicated, may hold values from 0 to 1151
- coupling: bfloat16 [1152, 1152], replicated, may hold values from -0.1875 to 0.1875
- stokes_kernel: float32 [32, 1152], replicated, may hold values from -0.1875 to 0.1875
- ocean_flow: float32 [2, 16, 16, 256], P(None, None, None, 'comp'), may hold values from -4 to 4
Outputs:
- forecast: float32 [1152, 16, 256], P('comp', 'grp')
- ocean_state: float32 [2, 16, 16, 256], P(None, None, None, 'comp')
All inputs are finite; a program needn't handle non-finite values. No bound on the sum of `sea_mask` on one device may be relied on, other than what follows from the above.
Results may differ from a plain program's by a relative error of at most 0.0004.
Values sent between devices are 32-bit elements; how exact they have to be, the bound alone decides.
A program may use at most 64 MiB of HBM per device.

v0:
```python
import jax
import jax.numpy as jnp
from jax import lax
from jax.sharding import PartitionSpec as P

L = 16
STEPS = 2
SUB = 3


SOURCE_GAIN = 0.3
CURRENT_GAIN = 0.25
CORIOLIS = 0.3
VISCOSITY = 0.15
MIXING = 0.15


def extended(cells, sides, width):
    for axis, dim in sides:
        count = lax.axis_size(axis)
        ends = count - 1
        head = lax.slice_in_dim(cells, 0, width, axis=dim)
        tail = lax.slice_in_dim(cells, cells.shape[dim] - width, cells.shape[dim], axis=dim)
        cells = jnp.concatenate(
            [
                lax.ppermute(tail, axis, [(i, (i + 1) % count) for i in range(ends)]),
                cells,
                lax.ppermute(head, axis, [((i + 1) % count, i) for i in range(ends)]),
            ],
            axis=dim,
        )
    return cells


def upwind(padded, energy, speed_x, speed_y, wet_cells):
    westward = padded[:, 1:-1, :-2]
    eastward = padded[:, 1:-1, 2:]
    southward = padded[:, :-2, 1:-1]
    northward = padded[:, 2:, 1:-1]
    moved = (
        energy
        - jnp.maximum(speed_x, 0.0) * (energy - westward)
        - jnp.minimum(speed_x, 0.0) * (eastward - energy)
        - jnp.maximum(speed_y, 0.0) * (energy - southward)
        - jnp.minimum(speed_y, 0.0) * (northward - energy)
    )
    return moved * wet_cells


def wave_sources(points, quad_index, coupling, stokes_kernel, wet_flat):
    channels, rows_local, cols_local = points.shape
    columns = points.reshape(channels, rows_local * cols_local)
    for substep in range(SUB):
        first = jnp.take(columns, quad_index[0], axis=0)
        second = jnp.take(columns, quad_index[1], axis=0)
        third = jnp.take(columns, quad_index[2], axis=0)
        fourth = jnp.take(columns, quad_index[3], axis=0)
        interaction = (
            first * second * (third + fourth) - third * fourth * (first + second)
        ).astype(jnp.bfloat16)
        growth = jnp.dot(coupling, interaction, preferred_element_type=jnp.float32)
        columns = columns + wet_flat * (
            SOURCE_GAIN * growth / (1.0 + SOURCE_GAIN * jnp.abs(growth))
        )
    profile = jnp.dot(stokes_kernel, columns, precision=lax.Precision.HIGHEST)
    return (columns.reshape(points.shape), profile.reshape(2, L, rows_local, cols_local))


def laplace(padded, field):
    return (
        padded[:, 1:-1, 2:]
        + padded[:, 1:-1, :-2]
        + padded[:, 2:, 1:-1]
        + padded[:, :-2, 1:-1]
        - 4.0 * field
    )


def vertical(field):
    stacked = jnp.pad(field, ((1, 1), (0, 0), (0, 0)))
    return stacked[2:] + stacked[:-2] - 2.0 * field


def ocean_step(padded, flow, stokes):
    flow_x = flow[0]
    flow_y = flow[1]
    padded_x = padded[0]
    padded_y = padded[1]
    vortex = 0.5 * (padded_y[:, 1:-1, 2:] - padded_y[:, 1:-1, :-2]) - 0.5 * (
        padded_x[:, 2:, 1:-1] - padded_x[:, :-2, 1:-1]
    )
    drift_x = stokes[0]
    drift_y = stokes[1]
    new_x = (
        flow_x
        + CORIOLIS * (flow_y + drift_y)
        + vortex * drift_y
        + VISCOSITY * laplace(padded_x, flow_x)
        + MIXING * vertical(flow_x)
    )
    new_y = (
        flow_y
        - CORIOLIS * (flow_x + drift_x)
        - vortex * drift_x
        + VISCOSITY * laplace(padded_y, flow_y)
        + MIXING * vertical(flow_y)
    )
    return jnp.stack([new_x, new_y])


def local(spectrum, group_speed, sea_mask, quad_index, coupling, stokes_kernel, ocean_flow):
    rows_local = sea_mask.shape[0]
    cols_local = ocean_flow.shape[3]
    comp_place = lax.axis_index("comp")
    group_place = lax.axis_index("grp")
    wet_rows = (sea_mask == 1).astype(jnp.float32)
    wet_tile = lax.dynamic_slice_in_dim(wet_rows, comp_place * cols_local, cols_local, 1)
    wet_flat = wet_tile.reshape(1, rows_local * cols_local)
    flow = ocean_flow
    points = lax.all_to_all(spectrum, "comp", split_axis=2, concat_axis=0, tiled=True)
    for iteration in range(STEPS):
        top_level = lax.dynamic_slice_in_dim(flow[:, 0], group_place * rows_local, rows_local, 1)
        drift = CURRENT_GAIN * jnp.tanh(top_level)
        padded = extended(points, (("comp", 2), ("grp", 1)), 1)
        speed_x = group_speed[0][:, None, None] + drift[0][None]
        speed_y = group_speed[1][:, None, None] + drift[1][None]
        points = upwind(padded, points, speed_x, speed_y, wet_tile[None])
        points, stokes = wave_sources(points, quad_index, coupling, stokes_kernel, wet_flat)
        whole_stokes = lax.all_gather(stokes, "grp", axis=2, tiled=True)
        advance_padded = extended(flow, (("comp", 3),), 1)
        advance_padded = jnp.pad(advance_padded, ((0, 0), (0, 0), (1, 1), (0, 0)))
        result = ocean_step(advance_padded, flow, whole_stokes)
        flow = result
    energy = lax.all_to_all(points, "comp", split_axis=0, concat_axis=2, tiled=True)
    return (energy, flow)


def solution(mesh):
    in_specs = (
        P("comp", "grp", None),
        P(),
        P("grp", None),
        P(),
        P(),
        P(),
        P(None, None, None, "comp"),
    )
    out_specs = (P("comp", "grp", None), P(None, None, None, "comp"))
    return jax.shard_map(local, mesh=mesh, in_specs=in_specs, out_specs=out_specs, check_vma=False)
```

profile of v0, /device:TPU:13, one launch (start us, length us, event | category | flops | bytes accessed | tf_op | source)
XLA Modules:
  0.0 259.0 jit_solution(8949231536399757708)
XLA Ops:
  2.7 3.7 %collective-permute-start.4 = (f32[2,16,16,1]{3,2,1,0:T(8,128)}, f32[2,16,16,1]{3,2,1,0:T(8,128)}, u32[]{:S(2)}, u32[]{:S(2)}) collective-permute-start(f32[2,16,16,1]{3,2,1,0:T(8,128)} %get-tuple-element.33), channel_id=1, source_target_pairs={{0,2},{2,4},{4,6},{6,8},{8,10},{10,12},{12,14},{14,16},{16,18},{18... | collective-permute-start | bytes 6152 | tf_op jit(solution)/shard_map/ppermute | solution.py:26
  10.8 6.5 %all-to-all-start = ((f32[72,8,256]{0,1,2:T(8,128)}), f32[72,8,256]{0,1,2:T(8,128)}, u32[]{:S(2)}, u32[]{:S(2)}) async-start(f32[72,8,256]{0,1,2:T(8,128)} %copy.89), calls=%async_computation | async-start | bytes 2097152 | tf_op jit(solution)/shard_map/all_to_all | solution.py:120
  21.3 20.9 %all-to-all-done = f32[72,8,256]{0,1,2:T(8,128)} async-done(((f32[72,8,256]{0,1,2:T(8,128)}), f32[72,8,256]{0,1,2:T(8,128)}, u32[]{:S(2)}, u32[]{:S(2)}) %all-to-all-start) | async-done | bytes 589856 | tf_op jit(solution)/shard_map/all_to_all | solution.py:120
  46.8 3.6 %collective-permute-start = (f32[1152,8,1]{0,2,1:T(1,128)S(1)}, f32[1152,8,1]{0,2,1:T(1,128)S(1)}, u32[]{:S(2)}, u32[]{:S(2)}) collective-permute-start(f32[1152,8,1]{0,2,1:T(1,128)S(1)} %get-tuple-element.23), channel_id=1, source_target_pairs={{0,2},{2,4},{4,6},{6,8},{8,10},{10,12},{12,14},{14,16},{16,18},{18... | collective-permute-start | bytes 110600 | tf_op jit(solution)/shard_map/ppermute | solution.py:26
  56.6 3.1 %collective-permute-start.2 = (f32[1152,1,18]{0,2,1:T(8,128)S(1)}, f32[1152,1,18]{0,2,1:T(8,128)S(1)}, u32[]{:S(2)}, u32[]{:S(2)}) collective-permute-start(f32[1152,1,18]{0,2,1:T(8,128)S(1)} %get-tuple-element.19), channel_id=1, source_target_pairs={{0,1},{2,3},{4,5},{6,7},{8,9},{10,11},{12,13},{14,15},{16,17},{18,... | collective-permute-start | bytes 248840 | tf_op jit(solution)/shard_map/ppermute | solution.py:26
  61.9 3.4 %collective-permute-done.3 = f32[1152,1,18]{0,2,1:T(8,128)S(1)} collective-permute-done((f32[1152,1,18]{0,2,1:T(8,128)S(1)}, f32[1152,1,18]{0,2,1:T(8,128)S(1)}, u32[]{:S(2)}, u32[]{:S(2)}) %collective-permute-start.3) | collective-permute-done | bytes 82976 | tf_op jit(solution)/shard_map/ppermute | solution.py:28
  77.4 3.1 %gather_fusion = f32[1152,128]{1,0:T(8,128)} fusion(f32[1152,128]{1,0:T(8,128)S(1)} %copy.92, s32[2048]{0:T(1024)S(1)} %pad_clamp_fusion.3), kind=kCustom, calls=%fused_computation.clone | custom fusion | bytes 1184256 | tf_op jit(solution)/shard_map/jit(_take)/gather | solution.py:54
  80.5 5.1 %bitcast_add_fusion.5 = f32[1152,128]{0,1:T(8,128)} fusion(f32[1152,128]{0,1:T(8,128)} %bitcast.103, bf16[1152,1152]{1,0:T(8,128)(2,1)S(1)} %copy-done, f32[1152,128]{1,0:T(8,128)} %gather_fusion.3, f32[1152,128]{1,0:T(8,128)} %gather_fusion.2, f32[1152,128]{1,0:T(8,128)} %gather_fusion.1, f32[1152,128]{1,0:T(8,128)} %gather_fusion, f32[128]{0:T(128)} %mul.306, ...), kind=kOutput, calls=%fused_computation.83 | convolution fusion | flops 342540288 | bytes 6198272 | tf_op jit(solution)/shard_map/dot_general | solution.py:61
  96.2 3.1 %gather_fusion.4 = f32[1152,128]{1,0:T(8,128)} fusion(f32[1152,128]{1,0:T(8,128)S(1)} %copy.96, s32[2048]{0:T(1024)S(1)} %pad_clamp_fusion.3), kind=kCustom, calls=%fused_computation.4.clone | custom fusion | bytes 1184256 | tf_op jit(solution)/shard_map/jit(_take)/gather | solution.py:54
  99.3 5.1 %bitcast_add_fusion.4 = f32[1152,128]{0,1:T(8,128)} fusion(f32[1152,128]{0,1:T(8,128)} %bitcast_add_fusion.5, bf16[1152,1152]{1,0:T(8,128)(2,1)S(1)} %copy-done, f32[1152,128]{1,0:T(8,128)} %gather_fusion.7, f32[1152,128]{1,0:T(8,128)} %gather_fusion.6, f32[1152,128]{1,0:T(8,128)} %gather_fusion.5, f32[1152,128]{1,0:T(8,128)} %gather_fusion.4, ...), kind=kOutput, calls=%fused_computation.82 | convolution fusion | flops 342540288 | bytes 6198272 | tf_op jit(solution)/shard_map/dot_general | solution.py:61
  118.1 4.3 %bitcast_add_fusion.3 = f32[1152,128]{0,1:T(8,128)S(1)} fusion(f32[1152,128]{0,1:T(8,128)} %bitcast_add_fusion.4, bf16[1152,1152]{1,0:T(8,128)(2,1)S(1)} %copy-done, f32[1152,128]{1,0:T(8,128)} %gather_fusion.11, f32[1152,128]{1,0:T(8,128)} %gather_fusion.10, f32[1152,128]{1,0:T(8,128)} %gather_fusion.9, f32[1152,128]{1,0:T(8,128)} %gather_fusion.8, ...), kind=kOutput, calls=%fused_computation.81 | convolution fusion | flops 342540288 | bytes 6198272 | tf_op jit(solution)/shard_map/dot_general | solution.py:61
  123.9 3.3 %collective-permute-start.6 = (f32[1152,8,1]{0,2,1:T(1,128)}, f32[1152,8,1]{0,2,1:T(1,128)}, u32[]{:S(2)}, u32[]{:S(2)}) collective-permute-start(f32[1152,8,1]{0,2,1:T(1,128)} %get-tuple-element.21), channel_id=1, source_target_pairs={{0,2},{2,4},{4,6},{6,8},{8,10},{10,12},{12,14},{14,16},{16,18},{18... | collective-permute-start | bytes 110600 | tf_op jit(solution)/shard_map/ppermute | solution.py:26
  129.9 5.9 %all_gather.6 = f32[2,16,16,16]{3,2,1,0:T(8,128)S(1)} all-gather(f32[2,16,8,16]{3,2,1,0:T(8,128)} %reshape.50), channel_id=1, replica_groups=mesh['comp'=16,'grp'=2] {'grp'}, dimensions={2}, use_global_device_ids=true | all-gather | bytes 49152 | tf_op jit(solution)/shard_map/all_gather | solution.py:129
  144.6 3.8 %collective-permute-done.9 = f32[1152,1,18]{0,2,1:T(8,128)S(1)} collective-permute-done((f32[1152,1,18]{0,2,1:T(8,128)S(1)}, f32[1152,1,18]{0,2,1:T(8,128)S(1)}, u32[]{:S(2)}, u32[]{:S(2)}) %collective-permute-start.9) | collective-permute-done | bytes 82976 | tf_op jit(solution)/shard_map/ppermute | solution.py:28
  161.3 3.1 %gather_fusion.12 = f32[1152,128]{1,0:T(8,128)} fusion(f32[1152,128]{1,0:T(8,128)S(1)} %copy.104, s32[2048]{0:T(1024)S(1)} %pad_clamp_fusion.3), kind=kCustom, calls=%fused_computation.12.clone | custom fusion | bytes 1184256 | tf_op jit(solution)/shard_map/jit(_take)/gather | solution.py:54
  164.5 5.2 %bitcast_add_fusion.2 = f32[1152,128]{0,1:T(8,128)} fusion(f32[1152,128]{0,1:T(8,128)} %bitcast.101, bf16[1152,1152]{1,0:T(8,128)(2,1)S(1)} %copy-done, f32[1152,128]{1,0:T(8,128)} %gather_fusion.15, f32[1152,128]{1,0:T(8,128)} %gather_fusion.14, f32[1152,128]{1,0:T(8,128)} %gather_fusion.13, f32[1152,128]{1,0:T(8,128)} %gather_fusion.12, ...), kind=kOutput, calls=%fused_computation.80 | convolution fusion | flops 342540288 | bytes 6198272 | tf_op jit(solution)/shard_map/dot_general | solution.py:61
  183.4 5.2 %bitcast_add_fusion.1 = f32[1152,128]{0,1:T(8,128)} fusion(f32[1152,128]{0,1:T(8,128)} %bitcast_add_fusion.2, bf16[1152,1152]{1,0:T(8,128)(2,1)S(1)} %copy-done, f32[1152,128]{1,0:T(8,128)} %gather_fusion.19, f32[1152,128]{1,0:T(8,128)} %gather_fusion.18, f32[1152,128]{1,0:T(8,128)} %gather_fusion.17, f32[1152,128]{1,0:T(8,128)} %gather_fusion.16, ...), kind=kOutput, calls=%fused_computation.79 | convolution fusion | flops 342540288 | bytes 6198272 | tf_op jit(solution)/shard_map/dot_general | solution.py:61
  202.2 4.4 %bitcast_add_fusion = f32[1152,128]{0,1:T(8,128)S(1)} fusion(f32[1152,128]{0,1:T(8,128)} %bitcast_add_fusion.1, bf16[1152,1152]{1,0:T(8,128)(2,1)S(1)} %copy-done, f32[1152,128]{1,0:T(8,128)} %gather_fusion.23, f32[1152,128]{1,0:T(8,128)} %gather_fusion.22, f32[1152,128]{1,0:T(8,128)} %gather_fusion.21, f32[1152,128]{1,0:T(8,128)} %gather_fusion.20, ...), kind=kOutput, calls=%fused_computation.78 | convolution fusion | flops 342540288 | bytes 6198272 | tf_op jit(solution)/shard_map/dot_general | solution.py:61
  210.4 4.5 %reshape.324 = f32[16,1,9216]{2,1,0:T(1,128)} reshape(f32[1152,8,16]{2,1,0:T(8,128)} %copy.116) | data formatting | bytes 1179648
  214.9 6.5 %all-to-all-start.1 = ((f32[16,1,9216]{2,1,0:T(1,128)}), f32[16,1,9216]{2,1,0:T(1,128)}, u32[]{:S(2)}, u32[]{:S(2)}) async-start(f32[16,1,9216]{2,1,0:T(1,128)} %reshape.324), calls=%async_computation.1 | async-start | bytes 1179648 | tf_op jit(solution)/shard_map/all_to_all | solution.py:134
  221.5 3.5 %collective-permute-start.10 = (f32[2,16,16,1]{3,2,1,0:T(8,128)S(1)}, f32[2,16,16,1]{3,2,1,0:T(8,128)S(1)}, u32[]{:S(2)}, u32[]{:S(2)}) collective-permute-start(f32[2,16,16,1]{3,2,1,0:T(8,128)S(1)} %get-tuple-element.29), channel_id=1, source_target_pairs={{0,2},{2,4},{4,6},{6,8},{8,10},{10,12},{12,14},{14,16},{16,18},{18... | collective-permute-start | bytes 6152 | tf_op jit(solution)/shard_map/ppermute | solution.py:26
  226.9 10.6 %collective-permute-done.10 = f32[2,16,16,1]{3,2,1,0:T(8,128)S(1)} collective-permute-done((f32[2,16,16,1]{3,2,1,0:T(8,128)S(1)}, f32[2,16,16,1]{3,2,1,0:T(8,128)S(1)}, u32[]{:S(2)}, u32[]{:S(2)}) %collective-permute-start.10) | collective-permute-done | bytes 2080 | tf_op jit(solution)/shard_map/ppermute | solution.py:26
  240.3 4.7 %all_gather.7 = f32[2,16,16,16]{3,2,1,0:T(8,128)S(1)} all-gather(f32[2,16,8,16]{3,2,1,0:T(8,128)S(1)} %reshape.53), channel_id=1, replica_groups=mesh['comp'=16,'grp'=2] {'grp'}, dimensions={2}, use_global_device_ids=true | all-gather | bytes 49152 | tf_op jit(solution)/shard_map/all_gather | solution.py:129
  252.8 3.8 %copy.118 = f32[72,8,16,16]{0,3,2,1:T(8,128)} copy(f32[72,8,16,16]{3,1,0,2:T(8,128)} %bitcast.88) | data formatting | bytes 1179648 | tf_op jit(solution)/shard_map/all_to_all | solution.py:134
  (147 shorter events, 131.3 us)
Async XLA Ops:
  0.6 79.9 %copy-start = (bf16[1152,1152]{1,0:T(8,128)(2,1)S(1)}, bf16[1152,1152]{1,0:T(8,128)(2,1)}, u32[]{:S(2)}) copy-start(bf16[1152,1152]{1,0:T(8,128)(2,1)} %param.13) | copy-start | bytes 7962628
  0.6 18.1 %slice-start = ((f32[2,16,16,16]{3,2,1,0:T(8,128)}), f32[2,1,16,16]{3,2,1,0:T(8,128)S(1)}, s32[]{:S(2)}) async-start(f32[2,16,16,16]{3,2,1,0:T(8,128)} %param.15), calls=%async_computation.2 | async-start | bytes 32768 | tf_op jit(solution)/shard_map/slice | solution.py:122
  0.7 20.0 %copy-start.1 = (f32[2,16,16,16]{3,2,1,0:T(8,128)S(1)}, f32[2,16,16,16]{3,2,1,0:T(8,128)}, u32[]{:S(2)}) copy-start(f32[2,16,16,16]{3,2,1,0:T(8,128)} %param.15) | copy-start | bytes 98308
  2.7 49.6 %collective-permute-start.4 = (f32[2,16,16,1]{3,2,1,0:T(8,128)}, f32[2,16,16,1]{3,2,1,0:T(8,128)}, u32[]{:S(2)}, u32[]{:S(2)}) collective-permute-start(f32[2,16,16,1]{3,2,1,0:T(8,128)} %get-tuple-element.33), channel_id=1, source_target_pairs={{0,2},{2,4},{4,6},{6,8},{8,10},{10,12},{12,14},{14,16},{16,18},{18... | collective-permute-start | bytes 6152 | tf_op jit(solution)/shard_map/ppermute | solution.py:26
  6.4 45.9 %collective-permute-start.5 = (f32[2,16,16,1]{3,2,1,0:T(8,128)}, f32[2,16,16,1]{3,2,1,0:T(8,128)}, u32[]{:S(2)}, u32[]{:S(2)}) collective-permute-start(f32[2,16,16,1]{3,2,1,0:T(8,128)} %get-tuple-element.34), channel_id=1, source_target_pairs={{2,0},{4,2},{6,4},{8,6},{10,8},{12,10},{14,12},{16,14},{18,16},{20... | collective-permute-start | bytes 6152 | tf_op jit(solution)/shard_map/ppermute | solution.py:28
  10.8 31.5 %all-to-all-start = ((f32[72,8,256]{0,1,2:T(8,128)}), f32[72,8,256]{0,1,2:T(8,128)}, u32[]{:S(2)}, u32[]{:S(2)}) async-start(f32[72,8,256]{0,1,2:T(8,128)} %copy.89), calls=%async_computation | async-start | bytes 2097152 | tf_op jit(solution)/shard_map/all_to_all | solution.py:120
  18.8 46.5 %copy-start.10 = (f32[1152]{0:T(1024)}, f32[1152]{0:T(1024)S(1)}, u32[]{:S(2)}) copy-start(f32[1152]{0:T(1024)S(1)} %get-tuple-element.13) | copy-start | bytes 13828
  18.8 46.4 %copy-start.11 = (f32[1152]{0:T(1024)}, f32[1152]{0:T(1024)S(1)}, u32[]{:S(2)}) copy-start(f32[1152]{0:T(1024)S(1)} %get-tuple-element.14) | copy-start | bytes 13828
  46.7 18.6 %copy-start.13 = (f32[8,16]{1,0:T(8,128)S(1)}, f32[8,16]{1,0:T(8,128)}, u32[]{:S(2)}) copy-start(f32[8,16]{1,0:T(8,128)} %copy-done.12) | copy-start | bytes 1540
  46.7 18.6 %copy-start.15 = (f32[8,16]{1,0:T(8,128)S(1)}, f32[8,16]{1,0:T(8,128)}, u32[]{:S(2)}) copy-start(f32[8,16]{1,0:T(8,128)} %get-tuple-element.37) | copy-start | bytes 1540
  46.7 18.6 %copy-start.16 = (f32[8,16]{1,0:T(8,128)S(1)}, f32[8,16]{1,0:T(8,128)}, u32[]{:S(2)}) copy-start(f32[8,16]{1,0:T(8,128)} %get-tuple-element.38) | copy-start | bytes 1540
  46.8 6.9 %collective-permute-start = (f32[1152,8,1]{0,2,1:T(1,128)S(1)}, f32[1152,8,1]{0,2,1:T(1,128)S(1)}, u32[]{:S(2)}, u32[]{:S(2)}) collective-permute-start(f32[1152,8,1]{0,2,1:T(1,128)S(1)} %get-tuple-element.23), channel_id=1, source_target_pairs={{0,2},{2,4},{4,6},{6,8},{8,10},{10,12},{12,14},{14,16},{16,18},{18... | collective-permute-start | bytes 110600 | tf_op jit(solution)/shard_map/ppermute | solution.py:26
  50.4 6.2 %collective-permute-start.1 = (f32[1152,8,1]{0,2,1:T(1,128)S(1)}, f32[1152,8,1]{0,2,1:T(1,128)S(1)}, u32[]{:S(2)}, u32[]{:S(2)}) collective-permute-start(f32[1152,8,1]{0,2,1:T(1,128)S(1)} %get-tuple-element.24), channel_id=1, source_target_pairs={{2,0},{4,2},{6,4},{8,6},{10,8},{12,10},{14,12},{16,14},{18,16},{20... | collective-permute-start | bytes 110600 | tf_op jit(solution)/shard_map/ppermute | solution.py:28
  56.6 5.2 %collective-permute-start.2 = (f32[1152,1,18]{0,2,1:T(8,128)S(1)}, f32[1152,1,18]{0,2,1:T(8,128)S(1)}, u32[]{:S(2)}, u32[]{:S(2)}) collective-permute-start(f32[1152,1,18]{0,2,1:T(8,128)S(1)} %get-tuple-element.19), channel_id=1, source_target_pairs={{0,1},{2,3},{4,5},{6,7},{8,9},{10,11},{12,13},{14,15},{16,17},{18,... | collective-permute-start | bytes 248840 | tf_op jit(solution)/shard_map/ppermute | solution.py:26
  59.8 5.5 %collective-permute-start.3 = (f32[1152,1,18]{0,2,1:T(8,128)S(1)}, f32[1152,1,18]{0,2,1:T(8,128)S(1)}, u32[]{:S(2)}, u32[]{:S(2)}) collective-permute-start(f32[1152,1,18]{0,2,1:T(8,128)S(1)} %get-tuple-element.20), channel_id=1, source_target_pairs={{1,0},{3,2},{5,4},{7,6},{9,8},{11,10},{13,12},{15,14},{17,16},{19,... | collective-permute-start | bytes 248840 | tf_op jit(solution)/shard_map/ppermute | solution.py:28
  123.9 16.1 %collective-permute-start.6 = (f32[1152,8,1]{0,2,1:T(1,128)}, f32[1152,8,1]{0,2,1:T(1,128)}, u32[]{:S(2)}, u32[]{:S(2)}) collective-permute-start(f32[1152,8,1]{0,2,1:T(1,128)} %get-tuple-element.21), channel_id=1, source_target_pairs={{0,2},{2,4},{4,6},{6,8},{8,10},{10,12},{12,14},{14,16},{16,18},{18... | collective-permute-start | bytes 110600 | tf_op jit(solution)/shard_map/ppermute | solution.py:26
  127.2 12.8 %collective-permute-start.7 = (f32[1152,8,1]{0,2,1:T(1,128)}, f32[1152,8,1]{0,2,1:T(1,128)}, u32[]{:S(2)}, u32[]{:S(2)}) collective-permute-start(f32[1152,8,1]{0,2,1:T(1,128)} %get-tuple-element.22), channel_id=1, source_target_pairs={{2,0},{4,2},{6,4},{8,6},{10,8},{12,10},{14,12},{16,14},{18,16},{20... | collective-permute-start | bytes 110600 | tf_op jit(solution)/shard_map/ppermute | solution.py:28
  140.8 3.8 %collective-permute-start.8 = (f32[1152,1,18]{0,2,1:T(8,128)S(1)}, f32[1152,1,18]{0,2,1:T(8,128)S(1)}, u32[]{:S(2)}, u32[]{:S(2)}) collective-permute-start(f32[1152,1,18]{0,2,1:T(8,128)S(1)} %get-tuple-element.17), channel_id=1, source_target_pairs={{0,1},{2,3},{4,5},{6,7},{8,9},{10,11},{12,13},{14,15},{16,17},{18,... | collective-permute-start | bytes 248840 | tf_op jit(solution)/shard_map/ppermute | solution.py:26
  142.4 6.0 %collective-permute-start.9 = (f32[1152,1,18]{0,2,1:T(8,128)S(1)}, f32[1152,1,18]{0,2,1:T(8,128)S(1)}, u32[]{:S(2)}, u32[]{:S(2)}) collective-permute-start(f32[1152,1,18]{0,2,1:T(8,128)S(1)} %get-tuple-element.18), channel_id=1, source_target_pairs={{1,0},{3,2},{5,4},{7,6},{9,8},{11,10},{13,12},{15,14},{17,16},{19,... | collective-permute-start | bytes 248840 | tf_op jit(solution)/shard_map/ppermute | solution.py:28
  214.9 24.6 %copy-start.9 = (f32[32,1152]{1,0:T(8,128)S(1)}, f32[32,1152]{1,0:T(8,128)}, u32[]{:S(2)}) copy-start(f32[32,1152]{1,0:T(8,128)} %param.14) | copy-start | bytes 442372
  214.9 31.2 %all-to-all-start.1 = ((f32[16,1,9216]{2,1,0:T(1,128)}), f32[16,1,9216]{2,1,0:T(1,128)}, u32[]{:S(2)}, u32[]{:S(2)}) async-start(f32[16,1,9216]{2,1,0:T(1,128)} %reshape.324), calls=%async_computation.1 | async-start | bytes 1179648 | tf_op jit(solution)/shard_map/all_to_all | solution.py:134
  221.4 18.1 %copy-start.7 = (f32[1152,128]{0,1:T(8,128)S(1)}, f32[1152,128]{0,1:T(8,128)}, u32[]{:S(2)}) copy-start(f32[1152,128]{0,1:T(8,128)} %copy-done.6) | copy-start | bytes 1769476
  221.5 16.0 %collective-permute-start.10 = (f32[2,16,16,1]{3,2,1,0:T(8,128)S(1)}, f32[2,16,16,1]{3,2,1,0:T(8,128)S(1)}, u32[]{:S(2)}, u32[]{:S(2)}) collective-permute-start(f32[2,16,16,1]{3,2,1,0:T(8,128)S(1)} %get-tuple-element.29), channel_id=1, source_target_pairs={{0,2},{2,4},{4,6},{6,8},{8,10},{10,12},{12,14},{14,16},{16,18},{18... | collective-permute-start | bytes 6152 | tf_op jit(solution)/shard_map/ppermute | solution.py:26
  225.0 14.2 %collective-permute-start.11 = (f32[2,16,16,1]{3,2,1,0:T(8,128)S(1)}, f32[2,16,16,1]{3,2,1,0:T(8,128)S(1)}, u32[]{:S(2)}, u32[]{:S(2)}) collective-permute-start(f32[2,16,16,1]{3,2,1,0:T(8,128)S(1)} %get-tuple-element.30), channel_id=1, source_target_pairs={{2,0},{4,2},{6,4},{8,6},{10,8},{12,10},{14,12},{16,14},{18,16},{20... | collective-permute-start | bytes 6152 | tf_op jit(solution)/shard_map/ppermute | solution.py:28
  (19 other events, 110.9 us)
where the time goes:
time: 262 us; the launch traced here: 259 us
  local copies, waits for them, and re-layouts  115 us (44%)
  waiting for transfers between devices  44 us (17%)
  starting transfers between devices  42.2 us (16%)
  matrix products  30.6 us (12%)
  other arithmetic  15.3 us (6%)
  blocking collectives  10.7 us (4%)
    dot_general x6, matrix products, wave_sources(): growth = jnp.dot(coupling, interaction, preferred_element_type=jnp.float32)  29.2 us
    all_to_all x1, waiting for transfers between devices, local(): lax.all_to_all(spectrum, 'comp', split_axis=2, concat_axis=0, tiled=True)  20.9 us
    ppermute x6, starting transfers between devices, extended(): lax.ppermute(tail, axis, [(i, (i + 1) % count) for i in range(ends)])  18.9 us
    gather x6, local copies, waits for them, and re-layouts, wave_sources(): first = jnp.take(columns, quad_index[0], axis=0)  18.7 us
    gather x6, local copies, waits for them, and re-layouts, wave_sources(): fourth = jnp.take(columns, quad_index[3], axis=0)  18.6 us
    gather x6, local copies, waits for them, and re-layouts, wave_sources(): second = jnp.take(columns, quad_index[1], axis=0)  18.6 us
    gather x6, local copies, waits for them, and re-layouts, wave_sources(): third = jnp.take(columns, quad_index[2], axis=0)  18.5 us
    unnamed x60, local copies, waits for them, and re-layouts  14.5 us
  transfers between devices with their start and end apart: 14, of which 7 were waited for; matrix products, arithmetic and copies ran while one was open for 7% of the time, Pallas kernels for 0%

commit v1 on v0

--- a/solution.py
+++ b/solution.py
@@ -1,6 +1,8 @@
 import jax
 import jax.numpy as jnp
 from jax import lax
+from jax.experimental import pallas as pl
+from jax.experimental.pallas import tpu as pltpu
 from jax.sharding import PartitionSpec as P
 
 L = 16
@@ -47,22 +49,67 @@
     return moved * wet_cells
 
 
+def source_kernel(energy_ref, quad_ref, coupling_ref, stokes_ref, wet_ref, out_ref, profile_ref, onehot, parts, inter):
+    channels = energy_ref.shape[0]
+    quads = coupling_ref.shape[1]
+    chunk = onehot.shape[1] // 4
+    lane = 128
+    place = lax.broadcasted_iota(jnp.int32, (lane, channels), 1)
+    for start in range(0, quads, lane):
+        turned = jnp.transpose(quad_ref[:, start:start + lane])
+        for j in range(4):
+            row = j * chunk + start % chunk
+            hit = place == turned[:, j:j + 1]
+            onehot[start // chunk, row:row + lane, :] = jnp.where(hit, 1.0, 0.0).astype(jnp.bfloat16)
+    out_ref[...] = energy_ref[...]
+    points = energy_ref.shape[1]
+
+    def substep(_, carry):
+        energy = out_ref[...]
+        high = energy.astype(jnp.bfloat16)
+        parts[:, :points] = high
+        parts[:, points:] = (energy - high.astype(jnp.float32)).astype(jnp.bfloat16)
+        for c in range(quads // chunk):
+            both = jnp.dot(onehot[c], parts[...], preferred_element_type=jnp.float32)
+            taken = both[:, :points] + both[:, points:]
+            first, second, third, fourth = [taken[j * chunk:(j + 1) * chunk] for j in range(4)]
+            inter[c * chunk:(c + 1) * chunk, :] = (
+                first * second * (third + fourth) - third * fourth * (first + second)
+            ).astype(jnp.bfloat16)
+        growth = jnp.dot(coupling_ref[...], inter[...], preferred_element_type=jnp.float32)
+        out_ref[...] = out_ref[...] + wet_ref[...] * (
+            SOURCE_GAIN * growth / (1.0 + SOURCE_GAIN * jnp.abs(growth))
+        )
+        return carry
+
+    lax.fori_loop(0, SUB, substep, 0)
+    profile_ref[...] = jnp.dot(
+        stokes_ref[...], out_ref[...], precision=lax.Precision.HIGHEST, preferred_element_type=jnp.float32
+    )
+
+
 def wave_sources(points, quad_index, coupling, stokes_kernel, wet_flat):
     channels, rows_local, cols_local = points.shape
     columns = points.reshape(channels, rows_local * cols_local)
-    for substep in range(SUB):
-        first = jnp.take(columns, quad_index[0], axis=0)
-        second = jnp.take(columns, quad_index[1], axis=0)
-        third = jnp.take(columns, quad_index[2], axis=0)
-        fourth = jnp.take(columns, quad_index[3], axis=0)
-        interaction = (
-            first * second * (third + fourth) - third * fourth * (first + second)
-        ).astype(jnp.bfloat16)
-        growth = jnp.dot(coupling, interaction, preferred_element_type=jnp.float32)
-        columns = columns + wet_flat * (
-            SOURCE_GAIN * growth / (1.0 + SOURCE_GAIN * jnp.abs(growth))
-        )
-    profile = jnp.dot(stokes_kernel, columns, precision=lax.Precision.HIGHEST)
+    quads = coupling.shape[1]
+    chunk = 384 if quads % 384 == 0 else quads
+    vmem = pl.BlockSpec(memory_space=pltpu.VMEM)
+    lanes = columns.shape[1]
+    columns, profile = pl.pallas_call(
+        source_kernel,
+        out_shape=(
+            jax.ShapeDtypeStruct(columns.shape, jnp.float32),
+            jax.ShapeDtypeStruct((stokes_kernel.shape[0], lanes), jnp.float32),
+        ),
+        in_specs=[vmem] * 5,
+        out_specs=(vmem, vmem),
+        scratch_shapes=[
+            pltpu.VMEM((quads // chunk, 4 * chunk, channels), jnp.bfloat16),
+            pltpu.VMEM((channels, 2 * lanes), jnp.bfloat16),
+            pltpu.VMEM((quads, lanes), jnp.bfloat16),
+        ],
+        compiler_params=pltpu.CompilerParams(vmem_limit_bytes=48 * 1024 * 1024),
+    )(columns, jnp.concatenate([quad_index, quad_index]), coupling, stokes_kernel, wet_flat)
     return (columns.reshape(points.shape), profile.reshape(2, L, rows_local, cols_local))
 
 

time: 262 us -> 181 us (0.69)
  local copies, waits for them, and re-layouts: 115 us -> 36.5 us
  Pallas kernels: 0 us -> 33.8 us
  matrix products: 30.6 us -> 0 us
  waiting for transfers between devices: 44 us -> 40.4 us
    gather x24 -> x0, local copies, waits for them, and re-layouts: 74.5 us -> none  [the longest x6 18.7 us: wave_sources(): first = jnp.take(columns, quad_index[0], axis=0)]
    pallas_call x0 -> x2, Pallas kernels: none -> 33.8 us  [wave_sources(): pl.pallas_call(source_kernel, out_shape=(jax.ShapeDtypeStruct(columns.sha...]
    dot_general x8 -> x0, matrix products: 30.6 us -> none  [the longest x6 29.2 us: wave_sources(): growth = jnp.dot(coupling, interaction, preferred_element_type=jnp.float32)]
    add x4 -> x0, local copies, waits for them, and re-layouts: 5.16 us -> none  [wave_sources(): columns + wet_flat * (SOURCE_GAIN * growth / (1.0 + SOURCE_GAIN * jnp.abs...]
    all_to_all x1, waiting for transfers between devices: 20.9 us -> 16.8 us  [local(): lax.all_to_all(spectrum, 'comp', split_axis=2, concat_axis=0, tiled=True)]
    unnamed x60 -> x28, local copies, waits for them, and re-layouts: 14.5 us -> 13.3 us
  transfers between devices with their start and end apart: 14 -> 14, of which waited for: 7 -> 7; matrix products, arithmetic and copies ran while one was open for 7% -> 8% of each run, Pallas kernels for 0% -> 0%
where the time goes in v1:
time: 181 us; the launch traced here: 179 us
  starting transfers between devices  42.2 us (23%)
  waiting for transfers between devices  40.4 us (22%)
  local copies, waits for them, and re-layouts  36.5 us (20%)
  Pallas kernels  33.8 us (19%)
  other arithmetic  14.4 us (8%)
  blocking collectives  10.4 us (6%)
    pallas_call x2, Pallas kernels, wave_sources(): pl.pallas_call(source_kernel, out_shape=(jax.ShapeDtypeStruct(columns.sha...  33.8 us
    ppermute x6, starting transfers between devices, extended(): lax.ppermute(tail, axis, [(i, (i + 1) % count) for i in range(ends)])  18.9 us
    all_to_all x1, waiting for transfers between devices, local(): lax.all_to_all(spectrum, 'comp', split_axis=2, concat_axis=0, tiled=True)  16.8 us
    unnamed x28, local copies, waits for them, and re-layouts  13.3 us
    ppermute x6, waiting for transfers between devices, extended(): lax.ppermute(head, axis, [((i + 1) % count, i) for i in range(ends)])  11.9 us
    ppermute x6, waiting for transfers between devices, extended(): lax.ppermute(tail, axis, [(i, (i + 1) % count) for i in range(ends)])  11.7 us
    ppermute x6, starting transfers between devices, extended(): lax.ppermute(head, axis, [((i + 1) % count, i) for i in range(ends)])  10.4 us
    all_gather x2, blocking collectives, local(): whole_stokes = lax.all_gather(stokes, 'grp', axis=2, tiled=True)  10.4 us
  transfers between devices with their start and end apart: 14, of which 7 were waited for; matrix products, arithmetic and copies ran while one was open for 8% of the time, Pallas kernels for 0%

profile of v1, /device:TPU:13, one launch (start us, length us, event | category | flops | bytes accessed | tf_op | source)
XLA Modules:
  0.0 178.8 jit_solution(15658985337103149892)
XLA Ops:
  0.7 2.4 %copy.26 = f32[72,8,256]{0,1,2:T(8,128)} copy(f32[72,8,256]{2,1,0:T(8,128)} %param.7) | data formatting | bytes 1179648 | tf_op args[0]
  3.1 6.6 %all-to-all-start = ((f32[72,8,256]{0,1,2:T(8,128)}), f32[72,8,256]{0,1,2:T(8,128)}, u32[]{:S(2)}, u32[]{:S(2)}) async-start(f32[72,8,256]{0,1,2:T(8,128)} %copy.26), calls=%async_computation | async-start | bytes 2097152 | tf_op jit(solution)/shard_map/all_to_all | solution.py:167
  11.5 3.3 %collective-permute-start.4 = (f32[2,16,16,1]{3,2,1,0:T(8,128)}, f32[2,16,16,1]{3,2,1,0:T(8,128)S(1)}, u32[]{:S(2)}, u32[]{:S(2)}) collective-permute-start(f32[2,16,16,1]{3,2,1,0:T(8,128)} %get-tuple-element.36), channel_id=1, source_target_pairs={{0,2},{2,4},{4,6},{6,8},{8,10},{10,12},{12,14},{14,16},{16,18},{18... | collective-permute-start | bytes 6152 | tf_op jit(solution)/shard_map/ppermute | solution.py:28
  17.8 16.8 %all-to-all-done = f32[72,8,256]{0,1,2:T(8,128)} async-done(((f32[72,8,256]{0,1,2:T(8,128)}), f32[72,8,256]{0,1,2:T(8,128)}, u32[]{:S(2)}, u32[]{:S(2)}) %all-to-all-start) | async-done | bytes 589856 | tf_op jit(solution)/shard_map/all_to_all | solution.py:167
  34.6 2.8 %copy.28 = f32[16,72,8,16]{1,0,3,2:T(8,128)} copy(f32[16,72,8,16]{1,2,3,0:T(8,128)} %bitcast.2) | data formatting | bytes 1179648 | tf_op jit(solution)/shard_map/all_to_all | solution.py:167
  37.4 2.5 %all_to_all.29 = f32[1152,8,16]{0,2,1:T(8,128)} reshape(f32[16,72,8,16]{1,0,3,2:T(8,128)} %copy.28) | data formatting | bytes 1179648 | tf_op jit(solution)/shard_map/all_to_all | solution.py:167
  41.0 4.1 %collective-permute-start = (f32[1152,8,1]{0,2,1:T(1,128)S(1)}, f32[1152,8,1]{0,2,1:T(1,128)S(1)}, u32[]{:S(2)}, u32[]{:S(2)}) collective-permute-start(f32[1152,8,1]{0,2,1:T(1,128)S(1)} %get-tuple-element.26), channel_id=1, source_target_pairs={{0,2},{2,4},{4,6},{6,8},{8,10},{10,12},{12,14},{14,16},{16,18},{18... | collective-permute-start | bytes 110600 | tf_op jit(solution)/shard_map/ppermute | solution.py:28
  48.3 3.0 %collective-permute-done.1 = f32[1152,8,1]{0,2,1:T(1,128)S(1)} collective-permute-done((f32[1152,8,1]{0,2,1:T(1,128)S(1)}, f32[1152,8,1]{0,2,1:T(1,128)S(1)}, u32[]{:S(2)}, u32[]{:S(2)}) %collective-permute-start.1) | collective-permute-done | bytes 36896 | tf_op jit(solution)/shard_map/ppermute | solution.py:30
  52.3 3.1 %collective-permute-start.2 = (f32[1152,1,18]{0,2,1:T(8,128)S(1)}, f32[1152,1,18]{0,2,1:T(8,128)S(1)}, u32[]{:S(2)}, u32[]{:S(2)}) collective-permute-start(f32[1152,1,18]{0,2,1:T(8,128)S(1)} %get-tuple-element.22), channel_id=1, source_target_pairs={{0,1},{2,3},{4,5},{6,7},{8,9},{10,11},{12,13},{14,15},{16,17},{18,... | collective-permute-start | bytes 248840 | tf_op jit(solution)/shard_map/ppermute | solution.py:28
  57.5 3.4 %collective-permute-done.3 = f32[1152,1,18]{0,2,1:T(8,128)S(1)} collective-permute-done((f32[1152,1,18]{0,2,1:T(8,128)S(1)}, f32[1152,1,18]{0,2,1:T(8,128)S(1)}, u32[]{:S(2)}, u32[]{:S(2)}) %collective-permute-start.3) | collective-permute-done | bytes 82976 | tf_op jit(solution)/shard_map/ppermute | solution.py:30
  60.9 3.7 %fusion.5 = f32[1152,8,16]{0,2,1:T(8,128)} fusion(f32[1152,8,16]{0,2,1:T(8,128)} %all_to_all.29, f32[1152,1,18]{0,2,1:T(8,128)S(1)} %collective-permute-done.3, f32[1152,8,1]{0,2,1:T(1,128)S(1)} %collective-permute-done.1, f32[1152,8,1]{0,2,1:T(1,128)S(1)} %collective-permute-done, f32[1152,1,18]{0,2,1:T(8,128)S(1)} %collective-permute-done.2, ...), kind=kLoop, calls=%fused_computation.15 | loop fusion | flops 3981312 | bytes 1430016 | tf_op jit(solution)/shard_map/mul | solution.py:49
  65.8 16.9 %shard_map.86 = (f32[1152,128]{1,0:T(8,128)S(1)}, f32[32,128]{1,0:T(8,128)S(1)}) custom-call(f32[1152,128]{1,0:T(8,128)S(1)} %copy.29.energy_ref, s32[8,1152]{1,0:T(8,128)S(1)} %pad_add_fusion.quad_ref, bf16[1152,1152]{1,0:T(8,128)(2,1)S(1)} %copy-done, f32[32,1152]{1,0:T(8,128)S(1)} %copy-done.1, f32[1,128]{1,0:T(1,128)S(1)} %reshape.45.wet_ref), custom_call_target="tpu_custom_call" | custom-call | tf_op jit(solution)/shard_map/pallas_call | solution.py:98
  85.6 3.3 %collective-permute-start.6 = (f32[1152,8,1]{0,2,1:T(1,128)}, f32[1152,8,1]{0,2,1:T(1,128)S(1)}, u32[]{:S(2)}, u32[]{:S(2)}) collective-permute-start(f32[1152,8,1]{0,2,1:T(1,128)} %get-tuple-element.24), channel_id=1, source_target_pairs={{0,2},{2,4},{4,6},{6,8},{8,10},{10,12},{12,14},{14,16},{16,18},{18... | collective-permute-start | bytes 110600 | tf_op jit(solution)/shard_map/ppermute | solution.py:28
  91.6 5.6 %all_gather.6 = f32[2,16,16,16]{3,2,1,0:T(8,128)S(1)} all-gather(f32[2,16,8,16]{3,2,1,0:T(8,128)} %reshape.47), channel_id=1, replica_groups=mesh['comp'=16,'grp'=2] {'grp'}, dimensions={2}, use_global_device_ids=true | all-gather | bytes 49152 | tf_op jit(solution)/shard_map/all_gather | solution.py:176
  105.5 3.8 %collective-permute-done.9 = f32[1152,1,18]{0,2,1:T(8,128)S(1)} collective-permute-done((f32[1152,1,18]{0,2,1:T(8,128)S(1)}, f32[1152,1,18]{0,2,1:T(8,128)S(1)}, u32[]{:S(2)}, u32[]{:S(2)}) %collective-permute-start.9) | collective-permute-done | bytes 82976 | tf_op jit(solution)/shard_map/ppermute | solution.py:30
  112.1 16.9 %shard_map.87 = (f32[1152,128]{1,0:T(8,128)S(1)}, f32[32,128]{1,0:T(8,128)S(1)}) custom-call(f32[1152,128]{1,0:T(8,128)S(1)} %copy.31.energy_ref, s32[8,1152]{1,0:T(8,128)S(1)} %pad_add_fusion.quad_ref, bf16[1152,1152]{1,0:T(8,128)(2,1)S(1)} %copy-done, f32[32,1152]{1,0:T(8,128)S(1)} %copy-done.1, f32[1,128]{1,0:T(1,128)S(1)} %reshape.45.wet_ref), custom_call_target="tpu_custom_call" | custom-call | tf_op jit(solution)/shard_map/pallas_call | solution.py:98
  131.2 3.0 %copy.33 = f32[1152,8,16]{2,1,0:T(8,128)} copy(f32[1152,8,16]{0,2,1:T(8,128)S(1)} %bitcast.74) | data formatting | bytes 1179648 | tf_op jit(solution)/shard_map/reshape | solution.py:113
  134.2 4.4 %reshape.53 = f32[16,1,9216]{2,1,0:T(1,128)} reshape(f32[1152,8,16]{2,1,0:T(8,128)} %copy.33) | data formatting | bytes 1179648
  138.6 6.3 %all-to-all-start.1 = ((f32[16,1,9216]{2,1,0:T(1,128)}), f32[16,1,9216]{2,1,0:T(1,128)S(1)}, u32[]{:S(2)}, u32[]{:S(2)}) async-start(f32[16,1,9216]{2,1,0:T(1,128)} %reshape.53), calls=%async_computation.1 | async-start | bytes 1179648 | tf_op jit(solution)/shard_map/all_to_all | solution.py:181
  145.0 3.3 %collective-permute-start.10 = (f32[2,16,16,1]{3,2,1,0:T(8,128)S(1)}, f32[2,16,16,1]{3,2,1,0:T(8,128)S(1)}, u32[]{:S(2)}, u32[]{:S(2)}) collective-permute-start(f32[2,16,16,1]{3,2,1,0:T(8,128)S(1)} %get-tuple-element.32), channel_id=1, source_target_pairs={{0,2},{2,4},{4,6},{6,8},{8,10},{10,12},{12,14},{14,16},{16,18},{18... | collective-permute-start | bytes 6152 | tf_op jit(solution)/shard_map/ppermute | solution.py:28
  150.3 10.7 %collective-permute-done.10 = f32[2,16,16,1]{3,2,1,0:T(8,128)S(1)} collective-permute-done((f32[2,16,16,1]{3,2,1,0:T(8,128)S(1)}, f32[2,16,16,1]{3,2,1,0:T(8,128)S(1)}, u32[]{:S(2)}, u32[]{:S(2)}) %collective-permute-start.10) | collective-permute-done | bytes 2080 | tf_op jit(solution)/shard_map/ppermute | solution.py:28
  163.1 4.7 %all_gather.7 = f32[2,16,16,16]{3,2,1,0:T(8,128)S(1)} all-gather(f32[2,16,8,16]{3,2,1,0:T(8,128)S(1)} %reshape.50), channel_id=1, replica_groups=mesh['comp'=16,'grp'=2] {'grp'}, dimensions={2}, use_global_device_ids=true | all-gather | bytes 49152 | tf_op jit(solution)/shard_map/all_gather | solution.py:176
  171.5 3.1 %reshape.54 = f32[1152,8,16]{2,1,0:T(8,128)} reshape(f32[16,9216]{1,0:T(8,128)S(1)} %reduce.4) | data formatting | bytes 1179648
  174.6 3.0 %copy.34 = f32[16,72,8,16]{1,3,0,2:T(8,128)S(1)} copy(f32[16,72,8,16]{3,2,1,0:T(8,128)} %bitcast.61) | data formatting | bytes 1179648 | tf_op jit(solution)/shard_map/all_to_all | solution.py:181
  (75 shorter events, 40.9 us)
Async XLA Ops:
  0.6 16.3 %slice-start = ((f32[2,16,16,16]{3,2,1,0:T(8,128)}), f32[2,1,16,16]{3,2,1,0:T(8,128)S(1)}, s32[]{:S(2)}) async-start(f32[2,16,16,16]{3,2,1,0:T(8,128)} %param.13), calls=%async_computation.2 | async-start | bytes 32768 | tf_op jit(solution)/shard_map/slice | solution.py:169
  0.6 16.4 %copy-start.4 = (f32[2,16,16,16]{3,2,1,0:T(8,128)S(1)}, f32[2,16,16,16]{3,2,1,0:T(8,128)}, u32[]{:S(2)}) copy-start(f32[2,16,16,16]{3,2,1,0:T(8,128)} %param.13) | copy-start | bytes 98308
  0.7 16.1 %copy-start.11 = (s32[8,256]{1,0:T(8,128)S(1)}, s32[8,256]{1,0:T(8,128)}, u32[]{:S(2)}) copy-start(s32[8,256]{1,0:T(8,128)} %param.9) | copy-start | bytes 24580
  0.7 16.3 %copy-start.10 = (f32[2,1152]{1,0:T(2,128)S(1)}, f32[2,1152]{1,0:T(2,128)}, u32[]{:S(2)}) copy-start(f32[2,1152]{1,0:T(2,128)} %param.8) | copy-start | bytes 27652
  0.7 16.4 %copy-start.9 = (s32[4,1152]{1,0:T(4,128)S(1)}, s32[4,1152]{1,0:T(4,128)}, u32[]{:S(2)}) copy-start(s32[4,1152]{1,0:T(4,128)} %param.10) | copy-start | bytes 55300
  3.1 31.5 %all-to-all-start = ((f32[72,8,256]{0,1,2:T(8,128)}), f32[72,8,256]{0,1,2:T(8,128)}, u32[]{:S(2)}, u32[]{:S(2)}) async-start(f32[72,8,256]{0,1,2:T(8,128)} %copy.26), calls=%async_computation | async-start | bytes 2097152 | tf_op jit(solution)/shard_map/all_to_all | solution.py:167
  11.5 35.5 %collective-permute-start.4 = (f32[2,16,16,1]{3,2,1,0:T(8,128)}, f32[2,16,16,1]{3,2,1,0:T(8,128)S(1)}, u32[]{:S(2)}, u32[]{:S(2)}) collective-permute-start(f32[2,16,16,1]{3,2,1,0:T(8,128)} %get-tuple-element.36), channel_id=1, source_target_pairs={{0,2},{2,4},{4,6},{6,8},{8,10},{10,12},{12,14},{14,16},{16,18},{18... | collective-permute-start | bytes 6152 | tf_op jit(solution)/shard_map/ppermute | solution.py:28
  14.9 32.2 %collective-permute-start.5 = (f32[2,16,16,1]{3,2,1,0:T(8,128)}, f32[2,16,16,1]{3,2,1,0:T(8,128)}, u32[]{:S(2)}, u32[]{:S(2)}) collective-permute-start(f32[2,16,16,1]{3,2,1,0:T(8,128)} %get-tuple-element.37), channel_id=1, source_target_pairs={{2,0},{4,2},{6,4},{8,6},{10,8},{12,10},{14,12},{16,14},{18,16},{20... | collective-permute-start | bytes 6152 | tf_op jit(solution)/shard_map/ppermute | solution.py:30
  17.8 48.0 %copy-start = (bf16[1152,1152]{1,0:T(8,128)(2,1)S(1)}, bf16[1152,1152]{1,0:T(8,128)(2,1)}, u32[]{:S(2)}) copy-start(bf16[1152,1152]{1,0:T(8,128)(2,1)} %coupling_ref.3) | copy-start | bytes 7962628
  17.8 48.0 %copy-start.1 = (f32[32,1152]{1,0:T(8,128)S(1)}, f32[32,1152]{1,0:T(8,128)}, u32[]{:S(2)}) copy-start(f32[32,1152]{1,0:T(8,128)} %stokes_ref.3) | copy-start | bytes 442372
  41.0 7.3 %collective-permute-start = (f32[1152,8,1]{0,2,1:T(1,128)S(1)}, f32[1152,8,1]{0,2,1:T(1,128)S(1)}, u32[]{:S(2)}, u32[]{:S(2)}) collective-permute-start(f32[1152,8,1]{0,2,1:T(1,128)S(1)} %get-tuple-element.26), channel_id=1, source_target_pairs={{0,2},{2,4},{4,6},{6,8},{8,10},{10,12},{12,14},{14,16},{16,18},{18... | collective-permute-start | bytes 110600 | tf_op jit(solution)/shard_map/ppermute | solution.py:28
  45.1 6.2 %collective-permute-start.1 = (f32[1152,8,1]{0,2,1:T(1,128)S(1)}, f32[1152,8,1]{0,2,1:T(1,128)S(1)}, u32[]{:S(2)}, u32[]{:S(2)}) collective-permute-start(f32[1152,8,1]{0,2,1:T(1,128)S(1)} %get-tuple-element.27), channel_id=1, source_target_pairs={{2,0},{4,2},{6,4},{8,6},{10,8},{12,10},{14,12},{16,14},{18,16},{20... | collective-permute-start | bytes 110600 | tf_op jit(solution)/shard_map/ppermute | solution.py:30
  52.3 5.2 %collective-permute-start.2 = (f32[1152,1,18]{0,2,1:T(8,128)S(1)}, f32[1152,1,18]{0,2,1:T(8,128)S(1)}, u32[]{:S(2)}, u32[]{:S(2)}) collective-permute-start(f32[1152,1,18]{0,2,1:T(8,128)S(1)} %get-tuple-element.22), channel_id=1, source_target_pairs={{0,1},{2,3},{4,5},{6,7},{8,9},{10,11},{12,13},{14,15},{16,17},{18,... | collective-permute-start | bytes 248840 | tf_op jit(solution)/shard_map/ppermute | solution.py:28
  55.4 5.5 %collective-permute-start.3 = (f32[1152,1,18]{0,2,1:T(8,128)S(1)}, f32[1152,1,18]{0,2,1:T(8,128)S(1)}, u32[]{:S(2)}, u32[]{:S(2)}) collective-permute-start(f32[1152,1,18]{0,2,1:T(8,128)S(1)} %get-tuple-element.23), channel_id=1, source_target_pairs={{1,0},{3,2},{5,4},{7,6},{9,8},{11,10},{13,12},{15,14},{17,16},{19,... | collective-permute-start | bytes 248840 | tf_op jit(solution)/shard_map/ppermute | solution.py:30
  85.6 15.8 %collective-permute-start.6 = (f32[1152,8,1]{0,2,1:T(1,128)}, f32[1152,8,1]{0,2,1:T(1,128)S(1)}, u32[]{:S(2)}, u32[]{:S(2)}) collective-permute-start(f32[1152,8,1]{0,2,1:T(1,128)} %get-tuple-element.24), channel_id=1, source_target_pairs={{0,2},{2,4},{4,6},{6,8},{8,10},{10,12},{12,14},{14,16},{16,18},{18... | collective-permute-start | bytes 110600 | tf_op jit(solution)/shard_map/ppermute | solution.py:28
  88.9 12.4 %collective-permute-start.7 = (f32[1152,8,1]{0,2,1:T(1,128)}, f32[1152,8,1]{0,2,1:T(1,128)S(1)}, u32[]{:S(2)}, u32[]{:S(2)}) collective-permute-start(f32[1152,8,1]{0,2,1:T(1,128)} %get-tuple-element.25), channel_id=1, source_target_pairs={{2,0},{4,2},{6,4},{8,6},{10,8},{12,10},{14,12},{16,14},{18,16},{20... | collective-permute-start | bytes 110600 | tf_op jit(solution)/shard_map/ppermute | solution.py:30
  98.9 1.8 copy-start.5
  101.4 4.2 %collective-permute-start.8 = (f32[1152,1,18]{0,2,1:T(8,128)S(1)}, f32[1152,1,18]{0,2,1:T(8,128)S(1)}, u32[]{:S(2)}, u32[]{:S(2)}) collective-permute-start(f32[1152,1,18]{0,2,1:T(8,128)S(1)} %get-tuple-element.20), channel_id=1, source_target_pairs={{0,1},{2,3},{4,5},{6,7},{8,9},{10,11},{12,13},{14,15},{16,17},{18,... | collective-permute-start | bytes 248840 | tf_op jit(solution)/shard_map/ppermute | solution.py:28
  103.1 6.3 %collective-permute-start.9 = (f32[1152,1,18]{0,2,1:T(8,128)S(1)}, f32[1152,1,18]{0,2,1:T(8,128)S(1)}, u32[]{:S(2)}, u32[]{:S(2)}) collective-permute-start(f32[1152,1,18]{0,2,1:T(8,128)S(1)} %get-tuple-element.21), channel_id=1, source_target_pairs={{1,0},{3,2},{5,4},{7,6},{9,8},{11,10},{13,12},{15,14},{17,16},{19,... | collective-permute-start | bytes 248840 | tf_op jit(solution)/shard_map/ppermute | solution.py:30
  131.2 13.7 %copy-start.6 = (f32[16,16,16]{2,1,0:T(8,128)S(1)}, f32[16,16,16]{2,1,0:T(8,128)}, u32[]{:S(2)}) copy-start(f32[16,16,16]{2,1,0:T(8,128)} %copy-done.5) | copy-start | bytes 49156
  131.2 13.7 %copy-start.8 = (f32[16,16,16]{2,1,0:T(8,128)S(1)}, f32[16,16,16]{2,1,0:T(8,128)}, u32[]{:S(2)}) copy-start(f32[16,16,16]{2,1,0:T(8,128)} %copy-done.7) | copy-start | bytes 49156
  138.6 30.3 %all-to-all-start.1 = ((f32[16,1,9216]{2,1,0:T(1,128)}), f32[16,1,9216]{2,1,0:T(1,128)S(1)}, u32[]{:S(2)}, u32[]{:S(2)}) async-start(f32[16,1,9216]{2,1,0:T(1,128)} %reshape.53), calls=%async_computation.1 | async-start | bytes 1179648 | tf_op jit(solution)/shard_map/all_to_all | solution.py:181
  145.0 16.0 %collective-permute-start.10 = (f32[2,16,16,1]{3,2,1,0:T(8,128)S(1)}, f32[2,16,16,1]{3,2,1,0:T(8,128)S(1)}, u32[]{:S(2)}, u32[]{:S(2)}) collective-permute-start(f32[2,16,16,1]{3,2,1,0:T(8,128)S(1)} %get-tuple-element.32), channel_id=1, source_target_pairs={{0,2},{2,4},{4,6},{6,8},{8,10},{10,12},{12,14},{14,16},{16,18},{18... | collective-permute-start | bytes 6152 | tf_op jit(solution)/shard_map/ppermute | solution.py:28
  148.4 14.3 %collective-permute-start.11 = (f32[2,16,16,1]{3,2,1,0:T(8,128)S(1)}, f32[2,16,16,1]{3,2,1,0:T(8,128)S(1)}, u32[]{:S(2)}, u32[]{:S(2)}) collective-permute-start(f32[2,16,16,1]{3,2,1,0:T(8,128)S(1)} %get-tuple-element.33), channel_id=1, source_target_pairs={{2,0},{4,2},{6,4},{8,6},{10,8},{12,10},{14,12},{16,14},{18,16},{20... | collective-permute-start | bytes 6152 | tf_op jit(solution)/shard_map/ppermute | solution.py:30
  (3 other events, 2.3 us)

commit v2 on v1

v2 whole, which is shorter than its diff:
```python
import functools

import jax
import jax.numpy as jnp
from jax import lax
from jax.experimental import pallas as pl
from jax.experimental.pallas import tpu as pltpu
from jax.sharding import PartitionSpec as P

L = 16
STEPS = 2
SUB = 3


SOURCE_GAIN = 0.3
CURRENT_GAIN = 0.25
CORIOLIS = 0.3
VISCOSITY = 0.15
MIXING = 0.15


MESH = pl.DeviceIdType.MESH


def upwind(energy, westward, eastward, southward, northward, speed_x, speed_y, wet_cells):
    moved = (
        energy
        - jnp.maximum(speed_x, 0.0) * (energy - westward)
        - jnp.minimum(speed_x, 0.0) * (eastward - energy)
        - jnp.maximum(speed_y, 0.0) * (energy - southward)
        - jnp.minimum(speed_y, 0.0) * (northward - energy)
    )
    return moved * wet_cells


def shifted(values, step, axis):
    return pltpu.roll(values, step % values.shape[axis], axis)


def swap_blocks(values):
    count, lanes = values.shape[-2:]
    width = lanes // count
    down, across = values.ndim - 2, values.ndim - 1
    s = lax.broadcasted_iota(jnp.int32, values.shape, down)
    l = lax.broadcasted_iota(jnp.int32, values.shape, across) // width
    step = 1
    while step < count:
        s_bit, l_bit = (s // step) % 2, (l // step) % 2
        upper = shifted(shifted(values, -step, down), step * width, across)
        lower = shifted(shifted(values, step, down), -step * width, across)
        values = jnp.where(s_bit == l_bit, values, jnp.where(s_bit == 0, upper, lower))
        step *= 2
    return values


def greet(n, g, me, gp, everyone):
    barrier = pltpu.get_barrier_semaphore()
    others = range(1, n) if everyone else (1, n - 1)
    for i in others:
        pl.semaphore_signal(barrier, inc=1, device_id=(lax.rem(me + i, n), gp), device_id_type=MESH)
    for i in range(1, g):
        pl.semaphore_signal(barrier, inc=1, device_id=(me, lax.rem(gp + i, g)), device_id_type=MESH)
    pl.semaphore_wait(barrier, len(others) + g - 1)


def remote(src, dst, send, recv, device):
    return pltpu.make_async_remote_copy(
        src_ref=src, dst_ref=dst, send_sem=send, recv_sem=recv, device_id=device, device_id_type=MESH
    )


def enter_kernel(n, g, spectrum_ref, flow_ref, speed_ref, mask_ref, out_ref,
                 south, north, drift_out, drift_in, blocks, sends, recvs, halo_sems):
    me, gp = lax.axis_index("comp"), lax.axis_index("grp")
    kept, rows, cols = spectrum_ref.shape
    lanes = blocks.shape[2]
    levels = flow_ref.shape[0] // 2
    greet(n, g, me, gp, True)
    up, down = lax.rem(gp + 1, g), lax.rem(gp + g - 1, g)
    to_up = remote(spectrum_ref.at[:, rows - 1, :], south.at[:, rows - 1, :], halo_sems.at[0], halo_sems.at[1], (me, up))
    to_down = remote(spectrum_ref.at[:, 0, :], north.at[:, 0, :], halo_sems.at[2], halo_sems.at[3], (me, down))
    to_up.start()
    to_down.start()
    here = pl.ds(pl.multiple_of(gp * lanes, lanes), lanes)
    drift_out[0:1, :] = CURRENT_GAIN * jnp.tanh(flow_ref[0:1, here])
    drift_out[1:2, :] = CURRENT_GAIN * jnp.tanh(flow_ref[levels:levels + 1, here])
    drift_in[me] = drift_out[...]
    for i in range(1, n):
        peer = lax.rem(me + i, n)
        remote(drift_out, drift_in.at[me], sends.at[0, peer], recvs.at[0, me], (peer, gp)).start()
    energy = spectrum_ref[...]
    row = lax.broadcasted_iota(jnp.int32, energy.shape, 1)
    col = lax.broadcasted_iota(jnp.int32, energy.shape, 2)
    westward = jnp.where(col == 0, 0.0, shifted(energy, 1, 2))
    eastward = jnp.where(col == cols - 1, 0.0, shifted(energy, -1, 2))
    to_up.wait()
    to_down.wait()
    below = jnp.where(gp == 0, 0.0, 1.0) * south[:, rows - 1:rows, :]
    above = jnp.where(gp == g - 1, 0.0, 1.0) * north[:, 0:1, :]
    southward = jnp.where(row == 0, below, shifted(energy, 1, 1))
    northward = jnp.where(row == rows - 1, above, shifted(energy, -1, 1))
    for i in range(1, n):
        peer = lax.rem(me + i, n)
        remote(drift_out, drift_in.at[peer], sends.at[0, peer], recvs.at[0, peer], (peer, gp)).wait()
    wet = (mask_ref[...] == 1).astype(jnp.float32)
    for h in range(cols // lanes):
        part = slice(h * lanes, (h + 1) * lanes)
        drift_x = swap_blocks(drift_in[h * rows:(h + 1) * rows, 0, :])
        drift_y = swap_blocks(drift_in[h * rows:(h + 1) * rows, 1, :])
        moved = upwind(
            energy[:, :, part], westward[:, :, part], eastward[:, :, part],
            southward[:, :, part], northward[:, :, part],
            speed_ref[0] + drift_x[None], speed_ref[1] + drift_y[None], wet[None, :, part],
        )
        blocks[h * rows:(h + 1) * rows] = jnp.swapaxes(swap_blocks(moved), 0, 1)
    for i in range(1, n):
        peer = lax.rem(me + i, n)
        remote(blocks.at[peer], out_ref.at[me], sends.at[1, peer], recvs.at[1, me], (peer, gp)).start()
    out_ref[me] = blocks[me]
    for i in range(1, n):
        peer = lax.rem(me + i, n)
        remote(blocks.at[peer], out_ref.at[peer], sends.at[1, peer], recvs.at[1, peer], (peer, gp)).wait()


def column_upwind(height, energy, halo_ref, pick_ref, speed_ref, drift_ref, wet):
    rows = halo_ref.shape[0]
    width = rows // 2 - height
    lanes = energy.shape[1]
    place = lax.broadcasted_iota(jnp.int32, (1, lanes), 1)
    turned = jnp.transpose(halo_ref[...])
    sides = 2 * height
    lateral = jnp.dot(turned[:, :sides], pick_ref[:sides, :], precision=lax.Precision.HIGHEST, preferred_element_type=jnp.float32)
    polar = jnp.dot(turned[:, sides:rows], pick_ref[sides:rows, :], precision=lax.Precision.HIGHEST, preferred_element_type=jnp.float32)
    col = place % width
    westward = jnp.where(col == 0, lateral, shifted(energy, 1, 1))
    eastward = jnp.where(col == width - 1, lateral, shifted(energy, -1, 1))
    southward = jnp.where(place < width, polar, shifted(energy, width, 1))
    northward = jnp.where(place >= lanes - width, polar, shifted(energy, -width, 1))
    return upwind(
        energy, westward, eastward, southward, northward,
        speed_ref[:, 0:1] + drift_ref[0:1, :], speed_ref[:, 1:2] + drift_ref[1:2, :], wet,
    )


def source_kernel(advect, height, energy_ref, quad_ref, coupling_ref, stokes_ref, wet_ref, pick_ref, *refs):
    if advect:
        halo_ref, speed_ref, drift_ref, *refs = refs
        out_ref, profile_ref, onehot, parts, inter = refs
    else:
        out_ref, profile_ref, edge_ref, onehot, parts, inter = refs
    channels = energy_ref.shape[0]
    quads = coupling_ref.shape[1]
    chunk = onehot.shape[1] // 4
    lane = 128
    place = lax.broadcasted_iota(jnp.int32, (lane, channels), 1)
    for start in range(0, quads, lane):
        turned = jnp.transpose(quad_ref[:, start:start + lane])
        for j in range(4):
            row = j * chunk + start % chunk
            hit = place == turned[:, j:j + 1]
            onehot[start // chunk, row:row + lane, :] = jnp.where(hit, 1.0, 0.0).astype(jnp.bfloat16)
    points = energy_ref.shape[1]
    if advect:
        out_ref[...] = column_upwind(
            height, energy_ref[...], halo_ref, pick_ref, speed_ref, drift_ref, wet_ref[...]
        )
    else:
        out_ref[...] = energy_ref[...]

    def substep(_, carry):
        energy = out_ref[...]
        high = energy.astype(jnp.bfloat16)
        parts[:, :points] = high
        parts[:, points:] = (energy - high.astype(jnp.float32)).astype(jnp.bfloat16)
        for c in range(quads // chunk):
            both = jnp.dot(onehot[c], parts[...], preferred_element_type=jnp.float32)
            taken = both[:, :points] + both[:, points:]
            first, second, third, fourth = [taken[j * chunk:(j + 1) * chunk] for j in range(4)]
            inter[c * chunk:(c + 1) * chunk, :] = (
                first * second * (third + fourth) - third * fourth * (first + second)
            ).astype(jnp.bfloat16)
        growth = jnp.dot(coupling_ref[...], inter[...], preferred_element_type=jnp.float32)
        out_ref[...] = out_ref[...] + wet_ref[...] * (
            SOURCE_GAIN * growth / (1.0 + SOURCE_GAIN * jnp.abs(growth))
        )
        return carry

    lax.fori_loop(0, SUB, substep, 0)
    profile_ref[...] = jnp.dot(
        stokes_ref[...], out_ref[...], precision=lax.Precision.HIGHEST, preferred_element_type=jnp.float32
    )
    if not advect:
        edge_ref[...] = lax.dot_general(
            pick_ref[...], out_ref[...], (((1,), (1,)), ((), ())),
            precision=lax.Precision.HIGHEST, preferred_element_type=jnp.float32,
        )


def ocean_step(width, flow, west_flow, east_flow, stokes, first, last):
    levels = flow.shape[0] // 2
    size = flow.shape[1]
    place = lax.broadcasted_iota(jnp.int32, flow.shape, 1)
    col = place % width
    level = lax.broadcasted_iota(jnp.int32, (levels, size), 0)
    west_edge = jnp.where(first, 0.0, shifted(west_flow, 1 - width, 1))
    east_edge = jnp.where(last, 0.0, shifted(east_flow, width - 1, 1))
    west = jnp.where(col == 0, west_edge, shifted(flow, 1, 1))
    east = jnp.where(col == width - 1, east_edge, shifted(flow, -1, 1))
    south = jnp.where(place < width, 0.0, shifted(flow, width, 1))
    north = jnp.where(place >= size - width, 0.0, shifted(flow, -width, 1))
    lap = east + west + north + south - 4.0 * flow
    u, v = flow[:levels], flow[levels:]

    def vertical(field):
        higher = jnp.where(level == 0, 0.0, shifted(field, 1, 0))
        lower = jnp.where(level == levels - 1, 0.0, shifted(field, -1, 0))
        return lower + higher - 2.0 * field

    vortex = 0.5 * (east[levels:] - west[levels:]) - 0.5 * (north[:levels] - south[:levels])
    drift_x, drift_y = stokes[:levels], stokes[levels:]
    new_x = u + CORIOLIS * (v + drift_y) + vortex * drift_y + VISCOSITY * lap[:levels] + MIXING * vertical(u)
    new_y = v - CORIOLIS * (u + drift_x) - vortex * drift_x + VISCOSITY * lap[levels:] + MIXING * vertical(v)
    return new_x, new_y


def ocean_copies(n, g, me, gp, flow_ref, profile_ref, west_flow, east_flow, stokes_all, sems, psend, precv):
    right, left = lax.rem(me + 1, n), lax.rem(me + n - 1, n)
    starts = [
        remote(flow_ref, west_flow, sems.at[0], sems.at[1], (right, gp)),
        remote(flow_ref, east_flow, sems.at[2], sems.at[3], (left, gp)),
    ]
    waits = list(starts)
    for i in range(1, g):
        peer = lax.rem(gp + i, g)
        starts.append(remote(profile_ref, stokes_all.at[gp], psend.at[peer], precv.at[gp], (me, peer)))
        waits.append(remote(profile_ref, stokes_all.at[peer], psend.at[peer], precv.at[peer], (me, peer)))
    for copy in starts:
        copy.start()
    stokes_all[gp] = profile_ref[...]
    return waits


def middle_kernel(n, g, width, flow_ref, profile_ref, edge_ref, flow_out, drift_out, halo_out,
                  west_flow, east_flow, stokes_all, halo, sems, psend, precv, halo_sems):
    me, gp = lax.axis_index("comp"), lax.axis_index("grp")
    levels = flow_ref.shape[0] // 2
    lanes = profile_ref.shape[1]
    height = lanes // width
    greet(n, g, me, gp, False)
    right, left = lax.rem(me + 1, n), lax.rem(me + n - 1, n)
    up, down = lax.rem(gp + 1, g), lax.rem(gp + g - 1, g)
    a, b, c, d = height, 2 * height, 2 * height + width, 2 * height + 2 * width
    waits = ocean_copies(n, g, me, gp, flow_ref, profile_ref, west_flow, east_flow, stokes_all, sems, psend, precv)
    moves = [
        remote(edge_ref.at[a:b], halo.at[0:a], halo_sems.at[0], halo_sems.at[1], (right, gp)),
        remote(edge_ref.at[0:a], halo.at[a:b], halo_sems.at[2], halo_sems.at[3], (left, gp)),
        remote(edge_ref.at[c:d], halo.at[b:c], halo_sems.at[4], halo_sems.at[5], (me, up)),
        remote(edge_ref.at[b:c], halo.at[c:d], halo_sems.at[6], halo_sems.at[7], (me, down)),
    ]
    for copy in moves:
        copy.start()
    for copy in waits:
        copy.wait()
    stokes = jnp.concatenate([stokes_all[i] for i in range(g)], axis=1)
    new_x, new_y = ocean_step(width, flow_ref[...], west_flow[...], east_flow[...], stokes, me == 0, me == n - 1)
    flow_out[:levels, :] = new_x
    flow_out[levels:, :] = new_y
    here = pl.ds(pl.multiple_of(gp * lanes, lanes), lanes)
    drift_out[0:1, :] = CURRENT_GAIN * jnp.tanh(flow_out[0:1, here])
    drift_out[1:2, :] = CURRENT_GAIN * jnp.tanh(flow_out[levels:levels + 1, here])
    for copy in moves:
        copy.wait()
    halo_out[0:a, :] = jnp.where(me == 0, 0.0, halo[0:a, :])
    halo_out[a:b, :] = jnp.where(me == n - 1, 0.0, halo[a:b, :])
    halo_out[b:c, :] = jnp.where(gp == 0, 0.0, halo[b:c, :])
    halo_out[c:d, :] = jnp.where(gp == g - 1, 0.0, halo[c:d, :])


def exit_kernel(n, g, width, points_ref, flow_ref, profile_ref, out_ref, flow_out,
                west_flow, east_flow, stokes_all, blocks, sems, psend, precv, sends, recvs):
    me, gp = lax.axis_index("comp"), lax.axis_index("grp")
    levels = flow_ref.shape[0] // 2
    kept, rows, cols = out_ref.shape
    lanes = blocks.shape[2]
    greet(n, g, me, gp, True)
    waits = ocean_copies(n, g, me, gp, flow_ref, profile_ref, west_flow, east_flow, stokes_all, sems, psend, precv)
    for i in range(1, n):
        peer = lax.rem(me + i, n)
        remote(points_ref.at[peer], blocks.at[me], sends.at[peer], recvs.at[me], (peer, gp)).start()
    blocks[me] = points_ref[me]
    for copy in waits:
        copy.wait()
    stokes = jnp.concatenate([stokes_all[i] for i in range(g)], axis=1)
    new_x, new_y = ocean_step(width, flow_ref[...], west_flow[...], east_flow[...], stokes, me == 0, me == n - 1)
    flow_out[:levels, :] = new_x
    flow_out[levels:, :] = new_y
    for i in range(1, n):
        peer = lax.rem(me + i, n)
        remote(points_ref.at[peer], blocks.at[peer], sends.at[peer], recvs.at[peer], (peer, gp)).wait()
    for h in range(cols // lanes):
        turned = jnp.swapaxes(blocks[h * rows:(h + 1) * rows], 0, 1)
        out_ref[:, :, h * lanes:(h + 1) * lanes] = swap_blocks(turned)


VMEM = pltpu.VMEM
DMA = pltpu.SemaphoreType.DMA


def call(kernel, operands, outs, scratch, collective=None):
    whole = pl.BlockSpec(memory_space=pltpu.VMEM)
    extra = {} if collective is None else {"collective_id": collective, "has_side_effects": True}
    return pl.pallas_call(
        kernel,
        out_shape=tuple(jax.ShapeDtypeStruct(shape, jnp.float32) for shape in outs),
        in_specs=[whole] * len(operands),
        out_specs=(whole,) * len(outs),
        scratch_shapes=scratch,
        compiler_params=pltpu.CompilerParams(vmem_limit_bytes=48 * 1024 * 1024, **extra),
    )(*operands)


def local(spectrum, group_speed, sea_mask, quad_index, coupling, stokes_kernel, ocean_flow):
    f32 = jnp.float32
    n, g = lax.axis_size("comp"), lax.axis_size("grp")
    kept, rows, cols = spectrum.shape
    width = ocean_flow.shape[3]
    lanes = rows * width
    channels, quads = coupling.shape
    place = lax.axis_index("comp")
    flow = ocean_flow.reshape(2 * L, -1)
    deep, size = flow.shape
    own = lax.dynamic_slice_in_dim(group_speed, place * kept, kept, 1)
    own = jnp.broadcast_to(own[:, :, None, None], (2, kept, rows, lanes))
    wet_flat = (lax.dynamic_slice_in_dim(sea_mask, place * width, width, 1) == 1).astype(f32).reshape(1, lanes)
    quad = jnp.concatenate([quad_index, quad_index])
    lane = jnp.arange(lanes)
    rank = jnp.arange(rows)[:, None]
    across = jnp.arange(width)[:, None]
    pick = jnp.concatenate([
        lane == rank * width, lane == rank * width + width - 1, lane == across, lane == lanes - width + across,
    ]).astype(f32)
    edges = pick.shape[0]
    chunk = 384 if quads % 384 == 0 else quads
    work = [
        VMEM((quads // chunk, 4 * chunk, channels), jnp.bfloat16),
        VMEM((channels, 2 * lanes), jnp.bfloat16),
        VMEM((quads, lanes), jnp.bfloat16),
    ]
    sea = [VMEM((deep, size), f32), VMEM((deep, size), f32), VMEM((g, deep, lanes), f32)]

    (points,) = call(
        functools.partial(enter_kernel, n, g), (spectrum, flow, own, sea_mask), ((n, kept, lanes),),
        [VMEM((kept, rows, cols), f32), VMEM((kept, rows, cols), f32), VMEM((2, lanes), f32),
         VMEM((n, 2, lanes), f32), VMEM((n, kept, lanes), f32), DMA((2, n)), DMA((2, n)), DMA((4,))], 0,
    )
    fixed = (quad, coupling, stokes_kernel, wet_flat, pick)
    points, profile, edge = call(
        functools.partial(source_kernel, False, rows), (points.reshape(channels, lanes), *fixed),
        ((channels, lanes), (deep, lanes), (edges, channels)), work,
    )
    flow, drift, halo = call(
        functools.partial(middle_kernel, n, g, width), (flow, profile, edge),
        ((deep, size), (2, lanes), (edges, channels)),
        sea + [VMEM((edges, channels), f32), DMA((4,)), DMA((g,)), DMA((g,)), DMA((8,))], 1,
    )
    points, profile = call(
        functools.partial(source_kernel, True, rows), (points, *fixed, halo, group_speed.T, drift),
        ((channels, lanes), (deep, lanes)), work,
    )
    energy, flow = call(
        functools.partial(exit_kernel, n, g, width), (points.reshape(n, kept, lanes), flow, profile),
        ((kept, rows, cols), (deep, size)),
        sea + [VMEM((n, kept, lanes), f32), DMA((4,)), DMA((g,)), DMA((g,)), DMA((n,)), DMA((n,))], 2,
    )
    return (energy, flow.reshape(ocean_flow.shape))


def solution(mesh):
    in_specs = (
        P("comp", "grp", None),
        P(),
        P("grp", None),
        P(),
        P(),
        P(),
        P(None, None, None, "comp"),
    )
    out_specs = (P("comp", "grp", None), P(None, None, None, "comp"))
    return jax.shard_map(local, mesh=mesh, in_specs=in_specs, out_specs=out_specs, check_vma=False)
```

time: 181 us -> 98.9 us (0.55)
  Pallas kernels: 33.8 us -> 86.6 us
  starting transfers between devices: 42.2 us -> 0 us
  waiting for transfers between devices: 40.4 us -> 0 us
  local copies, waits for them, and re-layouts: 36.5 us -> 9.43 us
  other arithmetic: 14.4 us -> 1.73 us
  blocking collectives: 10.4 us -> 0 us
    pallas_call x2 -> x5, Pallas kernels: 33.8 us -> 86.6 us  [call(): pl.pallas_call(kernel, out_shape=tuple((jax.ShapeDtypeStruct(shape, jnp.f...]
    ppermute x12 -> x0, starting transfers between devices: 29.4 us -> none  [the longest x6 18.9 us: extended(): lax.ppermute(tail, axis, [(i, (i + 1) % count) for i in range(ends)])]
    ppermute x12 -> x0, waiting for transfers between devices: 23.6 us -> none  [the longest x6 11.9 us: extended(): lax.ppermute(head, axis, [((i + 1) % count, i) for i in range(ends)])]
    all_to_all x2 -> x0, waiting for transfers between devices: 16.8 us -> none  [the longest x1 16.8 us: local(): lax.all_to_all(spectrum, 'comp', split_axis=2, concat_axis=0, tiled=True)]
    all_to_all x2 -> x0, starting transfers between devices: 12.8 us -> none  [the longest x1 6.55 us: local(): lax.all_to_all(spectrum, 'comp', split_axis=2, concat_axis=0, tiled=True)]
    all_gather x2 -> x0, blocking collectives: 10.4 us -> none  [local(): whole_stokes = lax.all_gather(stokes, 'grp', axis=2, tiled=True)]
    all_to_all x4 -> x0, local copies, waits for them, and re-layouts: 8.78 us -> none  [the longest x2 5.24 us: local(): lax.all_to_all(spectrum, 'comp', split_axis=2, concat_axis=0, tiled=True)]
    unnamed x28 -> x20, local copies, waits for them, and re-layouts: 13.3 us -> 6.32 us
  transfers between devices with their start and end apart: 14 -> 0, of which waited for: 7 -> 0; matrix products, arithmetic and copies ran while one was open for 8% -> 0% of each run, Pallas kernels for 0% -> 0%
where the time goes in v2:
time: 98.9 us; the launch traced here: 98.5 us
  Pallas kernels  86.6 us (88%)
  local copies, waits for them, and re-layouts  9.43 us (10%)
  other arithmetic  1.73 us (2%)
    pallas_call x5, Pallas kernels, call(): pl.pallas_call(kernel, out_shape=tuple((jax.ShapeDtypeStruct(shape, jnp.f...  86.6 us
    unnamed x20, local copies, waits for them, and re-layouts  6.32 us

profile of v2, /device:TPU:13, one launch (start us, length us, event | category | flops | bytes accessed | tf_op | source)
XLA Modules:
  0.0 98.5 jit_solution(18247177505685028756)
XLA Ops:
  0.7 0.9 constant_dynamic-slice_fusion
  1.6 0.1 iota_compare_fusion.2
  1.7 0.8 fusion
  2.4 0.1 reshape.43.wet_ref
  2.5 0.1 iota_compare_fusion
  2.6 1.1 %reshape.36.flow_ref = f32[32,256]{1,0:T(8,128)S(1)} reshape(f32[2,16,16,16]{3,2,1,0:T(8,128)} %param.13) | data formatting | bytes 65536 | tf_op jit(solution)/shard_map/reshape | solution.py:330
  3.7 0.8 pad_add_fusion.quad_ref
  4.5 0.2 broadcast_in_dim.2.speed_ref
  4.7 0.0 copy-start.2
  4.7 1.1 %copy-done.2 = f32[72,8,256]{2,1,0:T(8,128)S(1)} copy-done((f32[72,8,256]{2,1,0:T(8,128)S(1)}, f32[72,8,256]{2,1,0:T(8,128)}, u32[]{:S(2)}) %copy-start.2) | copy-done | bytes 589848
  5.8 0.7 copy-done.7
  6.5 25.4 %shard_map.86 = f32[16,72,128]{2,1,0:T(8,128)S(1)} custom-call(f32[72,8,256]{2,1,0:T(8,128)S(1)} %copy-done.2, f32[32,256]{1,0:T(8,128)S(1)} %reshape.36.flow_ref, f32[2,72,8,128]{3,2,1,0:T(8,128)S(1)} %broadcast_in_dim.2.speed_ref, s32[8,256]{1,0:T(8,128)S(1)} %copy-done.7), custom_call_target="tpu_custom_call" | custom-call | tf_op jit(solution)/shard_map/pallas_call | solution.py:312
  31.9 17.6 %shard_map.87 = (f32[1152,128]{1,0:T(8,128)S(1)}, f32[32,128]{1,0:T(8,128)S(1)}, f32[48,1152]{1,0:T(8,128)S(1)}) custom-call(f32[1152,128]{1,0:T(8,128)S(1)} %bitcast.5, s32[8,1152]{1,0:T(8,128)S(1)} %pad_add_fusion.quad_ref, bf16[1152,1152]{1,0:T(8,128)(2,1)S(1)} %copy-done, f32[32,1152]{1,0:T(8,128)S(1)} %copy-done.1, f32[1,128]{1,0:T(1,128)S(1)} %reshape.43.wet_ref, ...), custom_call_target="tpu_custom_call" | custom-call | tf_op jit(solution)/shard_map/pallas_call | solution.py:312
  49.5 0.8 copy-done.3
  50.3 6.0 %shard_map.88 = (f32[32,256]{1,0:T(8,128)S(1)}, f32[2,128]{1,0:T(2,128)S(1)}, f32[48,1152]{1,0:T(8,128)S(1)}) custom-call(f32[32,256]{1,0:T(8,128)S(1)} %reshape.36.flow_ref, f32[32,128]{1,0:T(8,128)S(1)} %get-tuple-element.13.profile_ref, f32[48,1152]{1,0:T(8,128)S(1)} %get-tuple-element.14.edge_ref), custom_call_target="tpu_custom_call" | custom-call | tf_op jit(solution)/shard_map/pallas_call | solution.py:312
  56.4 0.7 copy-done.5
  57.0 0.2 copy.9
  57.3 0.0 copy-start.4
  57.3 1.1 %copy-done.4 = f32[1152,128]{1,0:T(8,128)S(1)} copy-done((f32[1152,128]{1,0:T(8,128)S(1)}, f32[1152,128]{1,0:T(8,128)}, u32[]{:S(2)}) %copy-start.4) | copy-done | bytes 589848
  58.4 0.9 copy-done.6
  59.3 18.3 %shard_map.89 = (f32[1152,128]{1,0:T(8,128)S(1)}, f32[32,128]{1,0:T(8,128)S(1)}) custom-call(f32[1152,128]{1,0:T(8,128)S(1)} %copy-done.4, s32[8,1152]{1,0:T(8,128)S(1)} %pad_add_fusion.quad_ref, bf16[1152,1152]{1,0:T(8,128)(2,1)S(1)} %copy-done, f32[32,1152]{1,0:T(8,128)S(1)} %copy-done.1, f32[1,128]{1,0:T(1,128)S(1)} %reshape.43.wet_ref, ...), custom_call_target="tpu_custom_call" | custom-call | tf_op jit(solution)/shard_map/pallas_call | solution.py:312
  77.6 19.2 %shard_map.90 = (f32[72,8,256]{2,1,0:T(8,128)S(1)}, f32[32,256]{1,0:T(8,128)S(1)}) custom-call(f32[16,72,128]{2,1,0:T(8,128)S(1)} %bitcast.7, f32[32,256]{1,0:T(8,128)S(1)} %get-tuple-element.18.flow_ref, f32[32,128]{1,0:T(8,128)S(1)} %get-tuple-element.19.profile_ref), custom_call_target="tpu_custom_call" | custom-call | tf_op jit(solution)/shard_map/pallas_call | solution.py:312
  96.8 0.8 reshape.41
  97.7 0.8 copy.11
  (14 shorter events, 0.0 us)
Async XLA Ops:
  0.6 31.3 %copy-start.1 = (f32[32,1152]{1,0:T(8,128)S(1)}, f32[32,1152]{1,0:T(8,128)}, u32[]{:S(2)}) copy-start(f32[32,1152]{1,0:T(8,128)} %stokes_ref.3) | copy-start | bytes 442372
  0.6 31.3 %copy-start = (bf16[1152,1152]{1,0:T(8,128)(2,1)S(1)}, bf16[1152,1152]{1,0:T(8,128)(2,1)}, u32[]{:S(2)}) copy-start(bf16[1152,1152]{1,0:T(8,128)(2,1)} %coupling_ref.3) | copy-start | bytes 7962628
  4.7 1.1 %copy-start.2 = (f32[72,8,256]{2,1,0:T(8,128)S(1)}, f32[72,8,256]{2,1,0:T(8,128)}, u32[]{:S(2)}) copy-start(f32[72,8,256]{2,1,0:T(8,128)} %spectrum_ref.1) | copy-start | bytes 1769476
  5.8 0.7 copy-start.7
  6.5 50.6 %copy-start.8 = (f32[2,1152]{1,0:T(2,128)S(1)}, f32[2,1152]{1,0:T(2,128)}, u32[]{:S(2)}) copy-start(f32[2,1152]{1,0:T(2,128)} %param.8) | copy-start | bytes 27652
  49.5 0.8 copy-start.3
  56.3 0.7 copy-start.5
  57.3 1.1 %copy-start.4 = (f32[1152,128]{1,0:T(8,128)S(1)}, f32[1152,128]{1,0:T(8,128)}, u32[]{:S(2)}) copy-start(f32[1152,128]{1,0:T(8,128)} %copy-done.3) | copy-start | bytes 1769476
  58.4 0.9 copy-start.6

commit v3 on v2

--- a/solution.py
+++ b/solution.py
@@ -122,15 +122,28 @@
         remote(blocks.at[peer], out_ref.at[peer], sends.at[1, peer], recvs.at[1, peer], (peer, gp)).wait()
 
 
-def column_upwind(height, energy, halo_ref, pick_ref, speed_ref, drift_ref, wet):
+def edge_pick(height, lanes):
+    width = lanes // height
+    shape = (2 * height + 2 * width, lanes)
+    k = lax.broadcasted_iota(jnp.int32, shape, 0)
+    east = (k - height) * width + width - 1
+    south = k - 2 * height
+    north = lanes - width + south - width
+    lane = jnp.where(
+        k < height, k * width, jnp.where(k < 2 * height, east, jnp.where(south < width, south, north))
+    )
+    return jnp.where(lax.broadcasted_iota(jnp.int32, shape, 1) == lane, 1.0, 0.0)
+
+
+def column_upwind(height, energy, halo_ref, pick, speed_ref, drift_ref, wet):
     rows = halo_ref.shape[0]
     width = rows // 2 - height
     lanes = energy.shape[1]
     place = lax.broadcasted_iota(jnp.int32, (1, lanes), 1)
     turned = jnp.transpose(halo_ref[...])
     sides = 2 * height
-    lateral = jnp.dot(turned[:, :sides], pick_ref[:sides, :], precision=lax.Precision.HIGHEST, preferred_element_type=jnp.float32)
-    polar = jnp.dot(turned[:, sides:rows], pick_ref[sides:rows, :], precision=lax.Precision.HIGHEST, preferred_element_type=jnp.float32)
+    lateral = jnp.dot(turned[:, :sides], pick[:sides], precision=lax.Precision.HIGHEST, preferred_element_type=jnp.float32)
+    polar = jnp.dot(turned[:, sides:rows], pick[sides:rows], precision=lax.Precision.HIGHEST, preferred_element_type=jnp.float32)
     col = place % width
     westward = jnp.where(col == 0, lateral, shifted(energy, 1, 1))
     eastward = jnp.where(col == width - 1, lateral, shifted(energy, -1, 1))
@@ -142,7 +155,7 @@
     )
 
 
-def source_kernel(advect, height, energy_ref, quad_ref, coupling_ref, stokes_ref, wet_ref, pick_ref, *refs):
+def source_kernel(advect, height, energy_ref, quad_ref, coupling_ref, stokes_ref, wet_ref, *refs):
     if advect:
         halo_ref, speed_ref, drift_ref, *refs = refs
         out_ref, profile_ref, onehot, parts, inter = refs
@@ -153,8 +166,10 @@
     chunk = onehot.shape[1] // 4
     lane = 128
     place = lax.broadcasted_iota(jnp.int32, (lane, channels), 1)
+    quad = jnp.concatenate([quad_ref[...], quad_ref[...]], axis=0)
+    pick = edge_pick(height, energy_ref.shape[1])
     for start in range(0, quads, lane):
-        turned = jnp.transpose(quad_ref[:, start:start + lane])
+        turned = jnp.transpose(quad[:, start:start + lane])
         for j in range(4):
             row = j * chunk + start % chunk
             hit = place == turned[:, j:j + 1]
@@ -162,7 +177,7 @@
     points = energy_ref.shape[1]
     if advect:
         out_ref[...] = column_upwind(
-            height, energy_ref[...], halo_ref, pick_ref, speed_ref, drift_ref, wet_ref[...]
+            height, energy_ref[...], halo_ref, pick, speed_ref, drift_ref, wet_ref[...]
         )
     else:
         out_ref[...] = energy_ref[...]
@@ -191,7 +206,7 @@
     )
     if not advect:
         edge_ref[...] = lax.dot_general(
-            pick_ref[...], out_ref[...], (((1,), (1,)), ((), ())),
+            pick, out_ref[...], (((1,), (1,)), ((), ())),
             precision=lax.Precision.HIGHEST, preferred_element_type=jnp.float32,
         )
 
@@ -315,7 +330,7 @@
         in_specs=[whole] * len(operands),
         out_specs=(whole,) * len(outs),
         scratch_shapes=scratch,
-        compiler_params=pltpu.CompilerParams(vmem_limit_bytes=48 * 1024 * 1024, **extra),
+        compiler_params=pltpu.CompilerParams(vmem_limit_bytes=(24 if collective is None else 16) * 1024 * 1024, **extra),
     )(*operands)
 
 
@@ -332,15 +347,8 @@
     own = lax.dynamic_slice_in_dim(group_speed, place * kept, kept, 1)
     own = jnp.broadcast_to(own[:, :, None, None], (2, kept, rows, lanes))
     wet_flat = (lax.dynamic_slice_in_dim(sea_mask, place * width, width, 1) == 1).astype(f32).reshape(1, lanes)
-    quad = jnp.concatenate([quad_index, quad_index])
-    lane = jnp.arange(lanes)
-    rank = jnp.arange(rows)[:, None]
-    across = jnp.arange(width)[:, None]
-    pick = jnp.concatenate([
-        lane == rank * width, lane == rank * width + width - 1, lane == across, lane == lanes - width + across,
-    ]).astype(f32)
-    edges = pick.shape[0]
-    chunk = 384 if quads % 384 == 0 else quads
+    edges = 2 * rows + 2 * width
+    chunk = 128 if quads % 128 == 0 else quads
     work = [
         VMEM((quads // chunk, 4 * chunk, channels), jnp.bfloat16),
         VMEM((channels, 2 * lanes), jnp.bfloat16),
@@ -353,7 +361,7 @@
         [VMEM((kept, rows, cols), f32), VMEM((kept, rows, cols), f32), VMEM((2, lanes), f32),
          VMEM((n, 2, lanes), f32), VMEM((n, kept, lanes), f32), DMA((2, n)), DMA((2, n)), DMA((4,))], 0,
     )
-    fixed = (quad, coupling, stokes_kernel, wet_flat, pick)
+    fixed = (quad_index, coupling, stokes_kernel, wet_flat)
     points, profile, edge = call(
         functools.partial(source_kernel, False, rows), (points.reshape(channels, lanes), *fixed),
         ((channels, lanes), (deep, lanes), (edges, channels)), work,

time: 98.9 us -> 95.9 us (0.970)
  Pallas kernels: 86.6 us -> 82.9 us
  local copies, waits for them, and re-layouts: 9.43 us -> 11.1 us
    pallas_call x5, Pallas kernels: 86.6 us -> 82.9 us  [call(): pl.pallas_call(kernel, out_shape=tuple((jax.ShapeDtypeStruct(shape, jnp.f...]
    unnamed x20 -> x26, local copies, waits for them, and re-layouts: 6.32 us -> 7.95 us
where the time goes in v3:
time: 95.9 us; the launch traced here: 95.5 us
  Pallas kernels  82.9 us (86%)
  local copies, waits for them, and re-layouts  11.1 us (12%)
    pallas_call x5, Pallas kernels, call(): pl.pallas_call(kernel, out_shape=tuple((jax.ShapeDtypeStruct(shape, jnp.f...  82.9 us
    unnamed x26, local copies, waits for them, and re-layouts  7.95 us

profile of v3, /device:TPU:13, one launch (start us, length us, event | category | flops | bytes accessed | tf_op | source)
XLA Modules:
  0.0 95.5 jit_solution(12657160738500544709)
XLA Ops:
  0.6 0.9 constant_dynamic-slice_fusion
  1.6 0.8 fusion
  2.3 0.1 reshape.29.wet_ref
  2.4 1.1 %reshape.22.flow_ref = f32[32,256]{1,0:T(8,128)S(1)} reshape(f32[2,16,16,16]{3,2,1,0:T(8,128)} %param.13) | data formatting | bytes 65536 | tf_op jit(solution)/shard_map/reshape | solution.py:345
  3.5 0.2 broadcast_in_dim.2.speed_ref
  3.7 0.0 copy-start.5
  3.7 1.1 %copy-done.5 = f32[72,8,256]{2,1,0:T(8,128)S(1)} copy-done((f32[72,8,256]{2,1,0:T(8,128)S(1)}, f32[72,8,256]{2,1,0:T(8,128)}, u32[]{:S(2)}) %copy-start.5) | copy-done | bytes 589848
  4.8 0.7 copy-done.10
  5.5 25.4 %shard_map.86 = f32[16,72,128]{2,1,0:T(8,128)S(1)} custom-call(f32[72,8,256]{2,1,0:T(8,128)S(1)} %copy-done.5, f32[32,256]{1,0:T(8,128)S(1)} %reshape.22.flow_ref, f32[2,72,8,128]{3,2,1,0:T(8,128)S(1)} %broadcast_in_dim.2.speed_ref, s32[8,256]{1,0:T(8,128)S(1)} %copy-done.10), custom_call_target="tpu_custom_call" | custom-call | tf_op jit(solution)/shard_map/pallas_call | solution.py:327
  30.9 0.9 copy-done.3
  31.9 0.7 copy-done.8
  32.6 15.8 %shard_map.87 = (f32[1152,128]{1,0:T(8,128)S(1)}, f32[32,128]{1,0:T(8,128)S(1)}, f32[48,1152]{1,0:T(8,128)S(1)}) custom-call(f32[1152,128]{1,0:T(8,128)S(1)} %bitcast.6, s32[4,1152]{1,0:T(4,128)S(1)} %copy-done.8, bf16[1152,1152]{1,0:T(8,128)(2,1)S(1)} %copy-done, f32[32,1152]{1,0:T(8,128)S(1)} %copy-done.3, f32[1,128]{1,0:T(1,128)S(1)} %reshape.29.wet_ref), custom_call_target="tpu_custom_call" | custom-call | tf_op jit(solution)/shard_map/pallas_call | solution.py:327
  48.4 0.0 copy-start.1
  48.4 0.8 copy-done.1
  49.2 6.0 %shard_map.88 = (f32[32,256]{1,0:T(8,128)S(1)}, f32[2,128]{1,0:T(2,128)S(1)}, f32[48,1152]{1,0:T(8,128)S(1)}) custom-call(f32[32,256]{1,0:T(8,128)S(1)} %reshape.22.flow_ref, f32[32,128]{1,0:T(8,128)S(1)} %get-tuple-element.13.profile_ref, f32[48,1152]{1,0:T(8,128)S(1)} %get-tuple-element.14.edge_ref), custom_call_target="tpu_custom_call" | custom-call | tf_op jit(solution)/shard_map/pallas_call | solution.py:327
  55.2 0.7 copy-done.6
  55.9 0.2 copy.9
  56.2 0.0 copy-start.2
  56.2 1.1 %copy-done.2 = f32[1152,128]{1,0:T(8,128)S(1)} copy-done((f32[1152,128]{1,0:T(8,128)S(1)}, f32[1152,128]{1,0:T(8,128)}, u32[]{:S(2)}) %copy-start.2) | copy-done | bytes 589848
  57.3 0.9 copy-done.7
  58.2 16.5 %shard_map.89 = (f32[1152,128]{1,0:T(8,128)S(1)}, f32[32,128]{1,0:T(8,128)S(1)}) custom-call(f32[1152,128]{1,0:T(8,128)S(1)} %copy-done.2, s32[4,1152]{1,0:T(4,128)S(1)} %copy-done.9, bf16[1152,1152]{1,0:T(8,128)(2,1)S(1)} %copy-done, f32[32,1152]{1,0:T(8,128)S(1)} %copy-done.4, f32[1,128]{1,0:T(1,128)S(1)} %reshape.29.wet_ref, f32[48,1152]{1,0:T(8,128)S(1)} %copy-done.7, ...), custom_call_target="tpu_custom_call" | custom-call | tf_op jit(solution)/shard_map/pallas_call | solution.py:327
  74.7 19.2 %shard_map.90 = (f32[72,8,256]{2,1,0:T(8,128)S(1)}, f32[32,256]{1,0:T(8,128)S(1)}) custom-call(f32[16,72,128]{2,1,0:T(8,128)S(1)} %bitcast.7, f32[32,256]{1,0:T(8,128)S(1)} %get-tuple-element.18.flow_ref, f32[32,128]{1,0:T(8,128)S(1)} %get-tuple-element.19.profile_ref), custom_call_target="tpu_custom_call" | custom-call | tf_op jit(solution)/shard_map/pallas_call | solution.py:327
  93.9 0.8 reshape.27
  94.7 0.8 copy.11
  (13 shorter events, 0.0 us)
Async XLA Ops:
  0.6 30.3 %copy-start = (bf16[1152,1152]{1,0:T(8,128)(2,1)S(1)}, bf16[1152,1152]{1,0:T(8,128)(2,1)}, u32[]{:S(2)}) copy-start(bf16[1152,1152]{1,0:T(8,128)(2,1)} %coupling_ref.3) | copy-start | bytes 7962628
  3.7 1.1 %copy-start.5 = (f32[72,8,256]{2,1,0:T(8,128)S(1)}, f32[72,8,256]{2,1,0:T(8,128)}, u32[]{:S(2)}) copy-start(f32[72,8,256]{2,1,0:T(8,128)} %spectrum_ref.1) | copy-start | bytes 1769476
  4.8 0.7 copy-start.10
  5.5 50.5 %copy-start.11 = (f32[2,1152]{1,0:T(2,128)S(1)}, f32[2,1152]{1,0:T(2,128)}, u32[]{:S(2)}) copy-start(f32[2,1152]{1,0:T(2,128)} %param.8) | copy-start | bytes 27652
  5.5 50.7 %copy-start.9 = (s32[4,1152]{1,0:T(4,128)S(1)}, s32[4,1152]{1,0:T(4,128)}, u32[]{:S(2)}) copy-start(s32[4,1152]{1,0:T(4,128)} %quad_ref.3) | copy-start | bytes 55300
  30.9 0.9 copy-start.3
  31.8 0.7 copy-start.8
  32.6 23.6 %copy-start.4 = (f32[32,1152]{1,0:T(8,128)S(1)}, f32[32,1152]{1,0:T(8,128)}, u32[]{:S(2)}) copy-start(f32[32,1152]{1,0:T(8,128)} %stokes_ref.3) | copy-start | bytes 442372
  48.4 0.8 copy-start.1
  55.2 0.7 copy-start.6
  56.2 1.1 %copy-start.2 = (f32[1152,128]{1,0:T(8,128)S(1)}, f32[1152,128]{1,0:T(8,128)}, u32[]{:S(2)}) copy-start(f32[1152,128]{1,0:T(8,128)} %copy-done.1) | copy-start | bytes 1769476
  57.3 0.9 copy-start.7
